TPU v7x, 256 devices: a whole 4x4x8 slice. The times are simulated.
256 devices in a mesh: dp: 64 (over y, z, core), tower: 2 (over x_hi), mp: 2 (over x_lo).
Axes of the slice: x: 4 (x_hi: 2, x_lo: 2; x = x_hi * 2 + x_lo), y: 4, z: 8, core: 2. Of those that a mesh axis runs over, the one named last changes fastest.
Arguments:
- inputs: bfloat16 [2, 16384, 1536], P('tower', 'dp'), may hold values from -6 to 6
- head_weight: bfloat16 [2, 1152, 1536], P('tower', None, 'mp'), may hold values from -0.15625 to 0.15625
- pair_index: int32 [16384], P('dp'), may hold values from 0 to 16383, as said below
Outputs:
- grad_head: float32 [2, 1152, 1536], P('tower', 'dp', 'mp')
- grad_in: bfloat16 [2, 16384, 1536], P('tower', 'dp', 'mp')
Inputs may be any that keep to these rules, and one draw needn't show every extreme that they name: Each aligned block of 256 entries is a permutation of that block's own indices: image i matches text pair_index[i], which lies in the same block.
All inputs are finite; a program needn't handle non-finite values.
Results may differ from a plain program's by a relative error of at most 0.019.
Values may be sent and summed in bfloat16 or wider, within the bound.
A program may use at most 128 MiB of HBM per device.

v0:
```python
import jax
import jax.numpy as jnp
from jax import lax
from jax.sharding import PartitionSpec as P

EPSILON = 1e-06
LOGIT_SCALE = 100.0
LOGIT_BIAS = -10.0
LOSS_SCALE = 16384.0


def from_partner(block, axis, stride):
    count = lax.axis_size(axis)
    route = []
    for low in range(count):
        high = low | 1 << stride
        if high != low and high < count:
            route += [(low, high), (high, low)]
    return lax.ppermute(block, axis, route)


def from_behind(block, axis, distance):
    devices = range(lax.axis_size(axis))
    route = [((i - distance) % len(devices), i) for i in devices]
    return lax.ppermute(block, axis, route)


def pair_grad(embedded, visitor, sign_grid, weight_pair):
    logits = (
        LOGIT_SCALE * jnp.einsum("re,ce->rc", embedded, visitor, preferred_element_type=jnp.float32)
        + LOGIT_BIAS
    )
    coeffs = (-weight_pair * sign_grid * jax.nn.sigmoid(-sign_grid * logits)).astype(jnp.bfloat16)
    return jnp.dot(coeffs, visitor, preferred_element_type=jnp.float32)


def shards(inputs, head_weight, pair_index):
    pooled = inputs[0]
    weight = head_weight[0]
    mp_count = lax.axis_size("mp")
    mp_index = lax.axis_index("mp")
    dp_count = lax.axis_size("dp")
    dp_index = lax.axis_index("dp")
    tower_index = lax.axis_index("tower")
    row_count = pooled.shape[0]
    half_width = weight.shape[1]
    half_rows = row_count // mp_count
    weight_pair = LOSS_SCALE * LOGIT_SCALE / (row_count * dp_count)
    pooled32 = pooled.astype(jnp.float32)
    scale_rms = jnp.sqrt(jnp.mean(pooled32 * pooled32, axis=-1, keepdims=True) + EPSILON)
    normed = (pooled32 / scale_rms).astype(jnp.bfloat16)
    normed_part = lax.dynamic_slice_in_dim(normed, mp_index * half_width, half_width, 1)
    partial_value = jnp.einsum("rd,ed->re", normed_part, weight, preferred_element_type=jnp.float32)
    projected = lax.psum(partial_value, "mp")
    inverse = lax.rsqrt(jnp.sum(projected * projected, axis=-1, keepdims=True) + EPSILON)
    unit = projected * inverse
    embedded = unit.astype(jnp.bfloat16)
    own_half = lax.dynamic_slice_in_dim(embedded, mp_index * half_rows, half_rows, 0)
    partner = from_partner(own_half, "tower", 0)
    row_ids = dp_index * row_count + jnp.arange(row_count, dtype=jnp.int32)
    column_base = dp_index * row_count + mp_index * half_rows

    def negative(visitor):
        return pair_grad(embedded, visitor, -1.0, weight_pair)

    local_cols = jnp.arange(half_rows, dtype=jnp.int32)
    image_match = pair_index[:, None] == (column_base + local_cols)[None, :]
    column_pos = jnp.take(pair_index, mp_index * half_rows + local_cols)
    text_match = column_pos[None, :] == row_ids[:, None]
    diag_signs = jnp.where(jnp.where(tower_index == 0, image_match, text_match), 1.0, -1.0).astype(
        jnp.float32
    )
    grad_unit = pair_grad(embedded, partner, diag_signs, weight_pair)

    def turn(counter, state_in):
        visitor, running = state_in
        visitor = from_behind(visitor, "dp", 1)
        return (visitor, running + negative(visitor))

    _, grad_unit = lax.fori_loop(0, dp_count - 1, turn, (partner, grad_unit))
    grad_unit = lax.psum(grad_unit.astype(jnp.bfloat16), "mp").astype(jnp.float32)
    dproj = (
        (grad_unit - unit * jnp.sum(unit * grad_unit, axis=-1, keepdims=True)) * inverse
    ).astype(jnp.bfloat16)
    local_grad = jnp.einsum("re,rd->ed", dproj, normed_part, preferred_element_type=jnp.float32)
    grad_weight = lax.psum_scatter(local_grad, "dp", scatter_dimension=0, tiled=True)
    dnormed = jnp.dot(dproj, weight, preferred_element_type=jnp.float32)
    grad_pooled = (dnormed / scale_rms).astype(jnp.bfloat16)
    return (grad_weight[None], grad_pooled[None])


def solution(mesh):
    in_specs = (P("tower", "dp", None), P("tower", None, "mp"), P("dp"))
    out_specs = (P("tower", "dp", "mp"), P("tower", "dp", "mp"))
    return jax.shard_map(shards, mesh=mesh, in_specs=in_specs, out_specs=out_specs, check_vma=False)
```

profile of v0, /device:TPU:5, one launch (start us, length us, event | category | flops | bytes accessed | tf_op | source)
XLA Modules:
  0.0 1072.6 jit_solution(5871716553698050761)
XLA Ops:
  13.8 55.5 %all-reduce.5.cloned.1.call-done = f32[256,1152]{1,0:T(8,128)} async-done(((f32[256,1152]{1,0:T(8,128)}), f32[256,1152]{1,0:T(8,128)}) %all-reduce.5.cloned.1.call-update) | async-done | bytes 1179664 | tf_op jit(solution)/shard_map/psum | solution.py:54
  84.2 714.1 %while.12 = (s32[]{:T(128)}, bf16[128,1152]{1,0:T(8,128)(2,1)S(1)}, f32[256,1152]{1,0:T(8,128)S(1)}, bf16[256,1152]{1,0:T(8,128)(2,1)}, s32[]{:T(128)}) while((s32[]{:T(128)}, bf16[128,1152]{1,0:T(8,128)(2,1)S(1)}, f32[256,1152]{1,0:T(8,128)S(1)}, bf16[256,1152]{1,0:T(8,128)(2,1)}, s32[]{:T(128)}) %tuple.26), condition=%wide.region_4.5_spmd, body=%wide.region_3.4_spmd.sunk | while | flops 151519232 | bytes 5013605 | solution.py:80
  180.5 9.5 collective-permute-done
  203.4 9.5 collective-permute-done
  226.2 9.5 collective-permute-done
  249.1 9.5 collective-permute-done
  272.0 9.5 collective-permute-done
  294.9 9.5 collective-permute-done
  317.8 9.5 collective-permute-done
  340.7 9.5 collective-permute-done
  363.6 9.5 collective-permute-done
  386.5 9.5 collective-permute-done
  615.3 9.5 collective-permute-done
  638.2 9.5 collective-permute-done
  661.1 9.5 collective-permute-done
  684.0 9.5 collective-permute-done
  706.9 9.5 collective-permute-done
  729.8 9.5 collective-permute-done
  752.7 9.5 collective-permute-done
  775.6 9.5 collective-permute-done
  799.3 43.0 %all-reduce.7.cloned.1.call-done = bf16[256,1152]{1,0:T(8,128)(2,1)} async-done(((bf16[256,1152]{1,0:T(8,128)(2,1)}), bf16[256,1152]{1,0:T(8,128)(2,1)}) %all-reduce.7.cloned.1.call-update) | async-done | bytes 589840 | tf_op jit(solution)/shard_map/psum | solution.py:81
  848.0 148.0 %fusion = f32[24,768]{1,0:T(8,128)S(1)} fusion(f32[1152,768]{1,0:T(8,128)} %fusion.60), kind=kCustom, calls=%all-reduce-scatter | all-reduce-scatter fusion | flops 1179649 | bytes 3613696
  1007.3 11.6 %collective-permute-start.14 = (f32[24,768]{1,0:T(8,128)S(1)}, f32[24,768]{1,0:T(8,128)S(1)}, u32[]{:S(2)}, u32[]{:S(2)}) collective-permute-start(f32[24,768]{1,0:T(8,128)S(1)} %fusion), channel_id=1, source_target_pairs={{0,52},{4,56},{8,60},{12,64},{16,68},{20,72},{24,76},{28,80},{32,8... | collective-permute-start | bytes 221192
  1055.0 10.1 concatenate
  (330 shorter events, 616.9 us)
Async XLA Ops:
  7.2 62.2 %all-reduce.5.cloned.1.call-start = ((), (), s32[]{:S(2)}) async-start(), calls=%async_computation | async-start | bytes 2359296 | tf_op jit(solution)/shard_map/psum | solution.py:54
  11.9 830.3 %all-reduce.7.cloned.1.call-start = ((), (), s32[]{:S(2)}) async-start(), calls=%async_computation.1 | async-start | bytes 1179648 | tf_op jit(solution)/shard_map/psum | solution.py:81
  111.7 9.5 collective-permute-start
  180.4 9.5 collective-permute-start
  203.3 9.5 collective-permute-start
  226.2 9.5 collective-permute-start
  615.3 9.5 collective-permute-start
  638.1 9.5 collective-permute-start
  661.0 9.5 collective-permute-start
  995.9 11.3 %collective-permute-start.17 = (f32[18,768]{1,0:T(8,128)S(1)}, f32[18,768]{1,0:T(8,128)S(1)}, u32[]{:S(2)}, u32[]{:S(2)}) collective-permute-start(f32[18,768]{1,0:T(8,128)S(1)} %slice.2), channel_id=1, source_target_pairs={{0,64},{4,68},{8,72},{12,76},{16,80},{20,84},{24,88},{28,92},{32,9... | collective-permute-start | bytes 165896
  997.2 21.6 %collective-permute-start.10 = (f32[24,768]{1,0:T(8,128)S(1)}, f32[24,768]{1,0:T(8,128)S(1)}, u32[]{:S(2)}, u32[]{:S(2)}) collective-permute-start(f32[24,768]{1,0:T(8,128)S(1)} %fusion), channel_id=1, source_target_pairs={{0,36},{4,40},{8,44},{12,48},{16,52},{20,56},{24,60},{28,64},{32,6... | collective-permute-start | bytes 221192
  998.6 22.3 %collective-permute-start.11 = (f32[24,768]{1,0:T(8,128)S(1)}, f32[24,768]{1,0:T(8,128)S(1)}, u32[]{:S(2)}, u32[]{:S(2)}) collective-permute-start(f32[24,768]{1,0:T(8,128)S(1)} %fusion), channel_id=1, source_target_pairs={{0,40},{4,44},{8,48},{12,52},{16,56},{20,60},{24,64},{28,68},{32,7... | collective-permute-start | bytes 221192
  999.9 23.2 %collective-permute-start.12 = (f32[24,768]{1,0:T(8,128)S(1)}, f32[24,768]{1,0:T(8,128)S(1)}, u32[]{:S(2)}, u32[]{:S(2)}) collective-permute-start(f32[24,768]{1,0:T(8,128)S(1)} %fusion), channel_id=1, source_target_pairs={{0,44},{4,48},{8,52},{12,56},{16,60},{20,64},{24,68},{28,72},{32,7... | collective-permute-start | bytes 221192
  1001.2 25.0 %collective-permute-start.13 = (f32[24,768]{1,0:T(8,128)S(1)}, f32[24,768]{1,0:T(8,128)S(1)}, u32[]{:S(2)}, u32[]{:S(2)}) collective-permute-start(f32[24,768]{1,0:T(8,128)S(1)} %fusion), channel_id=1, source_target_pairs={{0,48},{4,52},{8,56},{12,60},{16,64},{20,68},{24,72},{28,76},{32,8... | collective-permute-start | bytes 221192
  1007.3 21.6 %collective-permute-start.14 = (f32[24,768]{1,0:T(8,128)S(1)}, f32[24,768]{1,0:T(8,128)S(1)}, u32[]{:S(2)}, u32[]{:S(2)}) collective-permute-start(f32[24,768]{1,0:T(8,128)S(1)} %fusion), channel_id=1, source_target_pairs={{0,52},{4,56},{8,60},{12,64},{16,68},{20,72},{24,76},{28,80},{32,8... | collective-permute-start | bytes 221192
  1018.9 14.1 %collective-permute-start.15 = (f32[24,768]{1,0:T(8,128)S(1)}, f32[24,768]{1,0:T(8,128)S(1)}, u32[]{:S(2)}, u32[]{:S(2)}) collective-permute-start(f32[24,768]{1,0:T(8,128)S(1)} %fusion), channel_id=1, source_target_pairs={{0,56},{4,60},{8,64},{12,68},{16,72},{20,76},{24,80},{28,84},{32,8... | collective-permute-start | bytes 221192
  1020.8 14.9 %collective-permute-start.16 = (f32[24,768]{1,0:T(8,128)S(1)}, f32[24,768]{1,0:T(8,128)S(1)}, u32[]{:S(2)}, u32[]{:S(2)}) collective-permute-start(f32[24,768]{1,0:T(8,128)S(1)} %fusion), channel_id=1, source_target_pairs={{0,60},{4,64},{8,68},{12,72},{16,76},{20,80},{24,84},{28,88},{32,9... | collective-permute-start | bytes 221192
  1023.0 17.4 %collective-permute-start.2 = (f32[24,768]{1,0:T(8,128)S(1)}, f32[24,768]{1,0:T(8,128)S(1)}, u32[]{:S(2)}, u32[]{:S(2)}) collective-permute-start(f32[24,768]{1,0:T(8,128)S(1)} %fusion), channel_id=1, source_target_pairs={{0,4},{4,8},{8,12},{12,16},{16,20},{20,24},{24,28},{28,32},{32,36}... | collective-permute-start | bytes 221192
  1026.1 17.4 %collective-permute-start.3 = (f32[24,768]{1,0:T(8,128)S(1)}, f32[24,768]{1,0:T(8,128)S(1)}, u32[]{:S(2)}, u32[]{:S(2)}) collective-permute-start(f32[24,768]{1,0:T(8,128)S(1)} %fusion), channel_id=1, source_target_pairs={{0,8},{4,12},{8,16},{12,20},{16,24},{20,28},{24,32},{28,36},{32,40... | collective-permute-start | bytes 221192
  1028.9 17.2 %collective-permute-start.4 = (f32[24,768]{1,0:T(8,128)S(1)}, f32[24,768]{1,0:T(8,128)S(1)}, u32[]{:S(2)}, u32[]{:S(2)}) collective-permute-start(f32[24,768]{1,0:T(8,128)S(1)} %fusion), channel_id=1, source_target_pairs={{0,12},{4,16},{8,20},{12,24},{16,28},{20,32},{24,36},{28,40},{32,4... | collective-permute-start | bytes 221192
  1033.0 20.6 %collective-permute-start.5 = (f32[24,768]{1,0:T(8,128)S(1)}, f32[24,768]{1,0:T(8,128)S(1)}, u32[]{:S(2)}, u32[]{:S(2)}) collective-permute-start(f32[24,768]{1,0:T(8,128)S(1)} %fusion), channel_id=1, source_target_pairs={{0,16},{4,20},{8,24},{12,28},{16,32},{20,36},{24,40},{28,44},{32,4... | collective-permute-start | bytes 221192
  1035.8 17.9 %collective-permute-start.6 = (f32[24,768]{1,0:T(8,128)S(1)}, f32[24,768]{1,0:T(8,128)S(1)}, u32[]{:S(2)}, u32[]{:S(2)}) collective-permute-start(f32[24,768]{1,0:T(8,128)S(1)} %fusion), channel_id=1, source_target_pairs={{0,20},{4,24},{8,28},{12,32},{16,36},{20,40},{24,44},{28,48},{32,5... | collective-permute-start | bytes 221192
  1040.5 13.2 %collective-permute-start.7 = (f32[24,768]{1,0:T(8,128)S(1)}, f32[24,768]{1,0:T(8,128)S(1)}, u32[]{:S(2)}, u32[]{:S(2)}) collective-permute-start(f32[24,768]{1,0:T(8,128)S(1)} %fusion), channel_id=1, source_target_pairs={{0,24},{4,28},{8,32},{12,36},{16,40},{20,44},{24,48},{28,52},{32,5... | collective-permute-start | bytes 221192
  1043.6 10.1 collective-permute-start.8
  (76 other events, 857.5 us)
Sparse Core Ops, SparseCore 0:
  12.0 57.2 all-reduce.4
  799.4 42.8 all-reduce.6
where the time goes:
time: 1080 us; the launch traced here: 1070 us
  waiting for transfers between devices  688 us (64%)
  blocking collectives  148 us (14%)
  matrix products  124 us (11%)
  starting transfers between devices  68.3 us (6%)
  local copies, waits for them, and re-layouts  19.3 us (2%)
  between operations  15.2 us (1%)
    ppermute x63, waiting for transfers between devices, from_behind(): return lax.ppermute(block, axis, route)  581 us
    unnamed x1, blocking collectives  148 us
    dot_general x64, matrix products, pair_grad(): return jnp.dot(coeffs, visitor, preferred_element_type=jnp.float32)  118 us
    psum x1, waiting for transfers between devices, shards(): projected = lax.psum(partial_value, 'mp')  55.5 us
    unnamed x16, starting transfers between devices  54.7 us
    psum x1, waiting for transfers between devices, shards(): lax.psum(grad_unit.astype(jnp.bfloat16), 'mp').astype(jnp.float32)  43 us
  transfers between devices with their start and end apart: 82, of which 66 were waited for; matrix products, arithmetic and copies ran while one was open for 0% of the time, Pallas kernels for 0%

commit v1 on v0

v1 whole, which is shorter than its diff:
```python
import jax
import jax.numpy as jnp
from jax import lax
from jax.experimental import pallas as pl
from jax.experimental.pallas import tpu as pltpu
from jax.sharding import PartitionSpec as P

EPSILON = 1e-06
LOGIT_SCALE = 100.0
LOGIT_BIAS = -10.0
BATCH = 16384
LOSS_SCALE = 16384.0
WEIGHT_PAIR = LOSS_SCALE * LOGIT_SCALE / BATCH
MAX_EXPONENT = 88.0
NX, NY, NZ = 4, 4, 8
ROWS = 256
OWN = 128
HALF = 64
QUARTER = 32
E = 1152
D = 1536
DH = 768
LANES = 384
EY = 288
F32 = jnp.float32
BF16 = jnp.bfloat16
MESH = pl.DeviceIdType.MESH
NT = (((1,), (1,)), ((), ()))
TN = (((0,), (0,)), ((), ()))


def dot(a, b, dims=(((1,), (0,)), ((), ()))):
    return lax.dot_general(a, b, dims, preferred_element_type=F32)


def kernel(
    pooled, weight, pairs, gw_out, gin_out,
    normed, rms_s, hsend, hrecv, proj, unit, inv_s, ebuf,
    img, txt, igrad, tgrad,
    sib_send, sib_recv, zsend, zrecv, yr1, yr2, xsend, xl_recv, xr_recv, ib_send, ib_recv,
    grad, dfull,
    local, c_send, c_recv, wy_send, wy_r1, wy_r2, wz_send, wz_recv, wc_send, wc_recv,
    h_sem, ix_sem, zr_sem, sb_sem, tx_sem, ty_sem, tf_sem,
    rsb_sem, rz_sem, ry1_sem, ry2_sem, rx_sem, rr_sem, ib_sem, dx_sem,
    c_sem, wy1_sem, wy2_sem, wz_sem, wc_sem,
):
    dp = lax.axis_index("dp")
    tower = lax.axis_index("tower")
    mp = lax.axis_index("mp")
    x = tower * 2 + mp
    y = dp // 16
    z = (dp // 2) % 8
    c = dp % 2

    def at(nx, ny, nz, nc):
        return {"dp": (ny * NZ + nz) * 2 + nc, "tower": nx // 2, "mp": nx % 2}

    xl = at(tower * 2 + 1 - mp, y, z, c)
    xr = at(3 - x, y, z, c)
    sib = at(x, y, z, 1 - c)
    yn = (at(x, (y + 1) % NY, z, c), at(x, (y + NY - 1) % NY, z, c))
    zs = [at(x, y, (z + d) % NZ, c) for d in range(NZ)]
    zn = (zs[1], zs[NZ - 1])
    is_home = x >= 2
    is_image = x < 2
    first = jnp.where(is_home, x - 2, 1 - x)
    second = 1 - first
    order = (first, second)

    peers = [xl, xr, sib, yn[0], yn[1]] + zs[1:]
    barrier = pltpu.get_barrier_semaphore()
    for peer in peers:
        pl.semaphore_signal(barrier, inc=1, device_id=peer, device_id_type=MESH)
    pl.semaphore_wait(barrier, len(peers))

    sent = []

    def copy(src, dst, sem, device):
        return pltpu.make_async_remote_copy(
            src_ref=src, dst_ref=dst, send_sem=sem.at[0], recv_sem=sem.at[1],
            device_id=device, device_id_type=MESH,
        )

    def send(src, dst, sem, device):
        step = copy(src, dst, sem, device)
        step.start()
        sent.append((None, step))

    def send_if(cond, src, dst, sem, device):
        step = copy(src, dst, sem, device)
        pl.when(cond)(step.start)
        sent.append((cond, step))

    def arrived(dst, sem):
        copy(dst, dst, sem, sib).wait_recv()

    def arrived_if(cond, dst, sem):
        pl.when(cond)(copy(dst, dst, sem, sib).wait_recv)

    full = pooled[0].astype(F32)
    rms = jnp.sqrt(jnp.mean(full * full, axis=-1, keepdims=True) + EPSILON)
    rms_s[...] = rms
    part = pooled[0, :, pl.ds(pl.multiple_of(mp * DH, DH), DH)].astype(F32)
    normed[...] = (part / rms).astype(BF16)
    theirs = pl.ds(pl.multiple_of((1 - mp) * OWN, OWN), OWN)
    mine = pl.ds(pl.multiple_of(mp * OWN, OWN), OWN)
    hsend[...] = dot(normed[theirs, :], weight[0], NT).astype(BF16).reshape(2, HALF, E)
    for j in (1, 0):
        send(hsend.at[j], hrecv.at[j], h_sem.at[j], xl)
    proj[...] = dot(normed[mine, :], weight[0], NT)

    def y_sends(a, j):
        xs = order[a]
        for way, slot in ((0, 3), (1, 1)):
            send(txt.at[0, xs, j], txt.at[slot, xs, j], ty_sem.at[a, j, way], yn[way])

    for j in (1, 0):
        arrived(hrecv.at[j], h_sem.at[j])
        rows = pl.ds(j * HALF, HALF)
        value = proj[rows, :] + hrecv[j].astype(F32)
        inverse = lax.rsqrt(jnp.sum(value * value, axis=-1, keepdims=True) + EPSILON)
        inv_s[rows, :] = inverse
        unit_j = value * inverse
        unit[rows, :] = unit_j
        embedded = unit_j.astype(BF16)

        @pl.when(is_home)
        def _():
            txt[0, first, j] = embedded

        @pl.when(is_image)
        def _():
            if j == 0:
                img[0, 0] = embedded.reshape(2, QUARTER, E)
            else:
                ebuf[...] = embedded.reshape(2, QUARTER, E)

        if j == 1:
            send_if(is_image, ebuf, img.at[0, 0], ix_sem, xr)
        send_if(is_home, txt.at[0, first, j], txt.at[0, first, j], tx_sem.at[j, 0], xr)

    def ring_sends(k):
        for way in (0, 1):
            slot = (NZ - k) % NZ if way == 0 else k
            for ch in (0, 1):
                if k == 3 and ch != way:
                    continue
                to = (slot - 1) % NZ if way == 0 else (slot + 1) % NZ
                send(img.at[slot, 0, ch], img.at[to, 0, ch], zr_sem.at[k, way, ch], zn[way])

    def ring_arrive(k):
        for ch in (0, 1):
            for way in (0, 1):
                if k == 4 and ch != way:
                    continue
                slot = (NZ - k) % NZ if way == 0 else k
                arrived(img.at[slot, 0, ch], zr_sem.at[k - 1, way, ch])
                if k < 4 and not (k == 3 and ch != way):
                    to = (slot - 1) % NZ if way == 0 else (slot + 1) % NZ
                    send(img.at[slot, 0, ch], img.at[to, 0, ch], zr_sem.at[k, way, ch], zn[way])
                send(img.at[slot, 0, ch], img.at[slot, 1, ch], sb_sem.at[slot, ch], sib)

    def own_image():
        ring_sends(0)
        for ch in (0, 1):
            send(img.at[0, 0, ch], img.at[0, 1, ch], sb_sem.at[0, ch], sib)

    for j in (1, 0):
        arrived_if(is_image, txt.at[0, first, j], tx_sem.at[j, 0])
        if j == 1:
            arrived_if(is_home, img.at[0, 0], ix_sem)
            own_image()
        send(txt.at[0, first, j], txt.at[0, first, j], tx_sem.at[j, 1], xl)
        y_sends(0, j)
    ring_arrive(1)
    for j in (1, 0):
        arrived(txt.at[0, second, j], tx_sem.at[j, 1])
        y_sends(1, j)
    ring_arrive(2)

    def y_forward(a):
        xs = order[a]
        for way, slot in ((0, 3), (1, 1)):
            for j in (1, 0):
                arrived(txt.at[slot, xs, j], ty_sem.at[a, j, way])
                if j == way:
                    send(txt.at[slot, xs, j], txt.at[2, xs, j], tf_sem.at[a, j], yn[way])

    y_forward(0)
    ring_arrive(3)
    y_forward(1)
    ring_arrive(4)
    for a in (0, 1):
        for j in (0, 1):
            arrived(txt.at[2, order[a], j], tf_sem.at[a, j])
    for slot in range(NZ):
        for ch in (0, 1):
            arrived(img.at[slot, 1, ch], sb_sem.at[slot, ch])

    source = jnp.where(is_image, x * OWN, (3 - x) * OWN + HALF)
    positions = pairs[pl.ds(pl.multiple_of(source, HALF), HALF), :] - dp * ROWS
    columns = lax.broadcasted_iota(jnp.int32, (HALF, ROWS), 1)
    igrad[...] = jnp.zeros_like(igrad)

    def visit(t, carry):
        images = img[...].reshape(NZ * OWN, E)
        texts = txt[t].reshape(ROWS, E)
        logits = LOGIT_SCALE * dot(images, texts, NT) + LOGIT_BIAS
        tail = WEIGHT_PAIR / (1.0 + jnp.exp(jnp.minimum(-logits[HALF:], MAX_EXPONENT)))
        match = jnp.logical_and(positions == columns, t == 0)
        sign = jnp.where(match, 1.0, -1.0)
        head = -WEIGHT_PAIR * sign / (1.0 + jnp.exp(jnp.minimum(sign * logits[:HALF], MAX_EXPONENT)))
        coeffs = jnp.concatenate([head, tail], axis=0).astype(BF16)
        igrad[...] += dot(coeffs, texts)
        tgrad[t] = dot(coeffs, images, TN).astype(BF16).reshape(2, 2, HALF, E)
        return carry

    lax.fori_loop(0, NY, visit, 0)

    for a in (1, 0):
        for way in (0, 1):
            send(tgrad.at[2, order[a], way], yr1.at[a, way], ry1_sem.at[a, way], yn[way])
    ahead = (4, 3, 5, 2, 6, 1, 7, 0)
    for slot in ahead:
        sib_send[slot] = igrad[pl.ds(slot * OWN + HALF, HALF), :].astype(BF16)
        send(sib_send.at[slot], sib_recv.at[slot], rsb_sem.at[slot], sib)
    for a in (1, 0):
        for way, slot in ((0, 1), (1, 3)):
            send(tgrad.at[slot, order[a], 1 - way], yr2.at[a, way, 1 - way], ry2_sem.at[a, way, 1 - way], yn[way])

    def z_send(way, far, ch):
        slot = far if way == 0 else NZ - far
        rows = pl.ds(slot * OWN + ch * QUARTER, QUARTER)
        value = igrad[rows, :] + sib_recv[slot, pl.ds(ch * QUARTER, QUARTER), :].astype(F32)
        if far < 3 or (far == 3 and ch == way):
            arrived(zrecv.at[way, far, ch], rz_sem.at[way, far, ch])
            value = value + zrecv[way, far, ch].astype(F32)
        zsend[way, far - 1, ch] = value.astype(BF16)
        send(zsend.at[way, far - 1, ch], zrecv.at[way, far - 1, ch], rz_sem.at[way, far - 1, ch], zn[way])

    def y_second(a):
        xs = order[a]
        for way, slot in ((0, 1), (1, 3)):
            arrived(yr1.at[a, way], ry1_sem.at[a, way])
            tgrad[slot, xs, way] = (tgrad[slot, xs, way].astype(F32) + yr1[a, way].astype(F32)).astype(BF16)
            send(tgrad.at[slot, xs, way], yr2.at[a, way, way], ry2_sem.at[a, way, way], yn[way])

    for slot in (4, 3, 5):
        arrived(sib_recv.at[slot], rsb_sem.at[slot])
    for way in (0, 1):
        z_send(way, 4, way)
    for way in (0, 1):
        z_send(way, 3, 1 - way)
    y_second(1)
    for slot in (2, 6, 1, 7, 0):
        arrived(sib_recv.at[slot], rsb_sem.at[slot])
    for way in (0, 1):
        z_send(way, 3, way)
    y_second(0)
    for far in (2, 1):
        for way in (0, 1):
            z_send(way, far, 1 - way)
        for way in (0, 1):
            z_send(way, far, way)

    def y_total(a, j):
        for way in (0, 1):
            arrived(yr2.at[a, way, j], ry2_sem.at[a, way, j])
        return tgrad[0, order[a], j].astype(F32) + yr2[a, 0, j].astype(F32) + yr2[a, 1, j].astype(F32)

    for j in (0, 1):
        xsend[1, j] = y_total(1, j).astype(BF16)
        send(xsend.at[1, j], xl_recv.at[j], rx_sem.at[j], xl)

    for ch in (0, 1):
        rows = pl.ds(ch * QUARTER, QUARTER)
        value = igrad[rows, :] + sib_recv[0, rows, :].astype(F32)
        for way in (0, 1):
            arrived(zrecv.at[way, 0, ch], rz_sem.at[way, 0, ch])
            value = value + zrecv[way, 0, ch].astype(F32)

        @pl.when(is_image)
        def _():
            grad[rows, :] = value

        @pl.when(is_home)
        def _():
            ib_send[ch] = value.astype(BF16)

        send_if(is_home, ib_send.at[ch], ib_recv.at[ch], ib_sem.at[ch], xr)

    for j in (0, 1):
        value = y_total(0, j)
        arrived(xl_recv.at[j], rx_sem.at[j])
        value = value + xl_recv[j].astype(F32)

        @pl.when(is_image)
        def _():
            xsend[0, j] = value.astype(BF16)

        send_if(is_image, xsend.at[0, j], xr_recv.at[j], rr_sem.at[j], xr)

        @pl.when(is_home)
        def _():
            grad[pl.ds(j * HALF, HALF), :] = value

    @pl.when(is_image)
    def _():
        for ch in (0, 1):
            arrived(ib_recv.at[ch], ib_sem.at[ch])
        grad[pl.ds(HALF, HALF), :] = ib_recv[...].astype(F32).reshape(HALF, E)

    @pl.when(is_home)
    def _():
        for j in (0, 1):
            arrived(xr_recv.at[j], rr_sem.at[j])
            rows = pl.ds(j * HALF, HALF)
            grad[rows, :] = grad[rows, :] + xr_recv[j].astype(F32)

    unit_v = unit[...]
    grad_v = grad[...]
    dproj = (grad_v - unit_v * jnp.sum(unit_v * grad_v, axis=-1, keepdims=True)) * inv_s[...]
    dfull[mp] = dproj.astype(BF16)
    send(dfull.at[mp], dfull.at[mp], dx_sem, xl)
    arrived(dfull.at[1 - mp], dx_sem)

    dproj_all = dfull[...].reshape(ROWS, E)
    local[...] = dot(dproj_all, normed[...], TN)

    theirs_l = pl.ds(pl.multiple_of((1 - c) * LANES, LANES), LANES)
    mine_l = pl.ds(pl.multiple_of(c * LANES, LANES), LANES)
    for r in (2, 1, 3, 0):
        rows = pl.ds(pl.multiple_of(((y + r) % NY) * EY, EY), EY)
        c_send[r] = local[rows, theirs_l].astype(BF16)
        send(c_send.at[r], c_recv.at[r], c_sem.at[r], sib)

    dnormed = dot(dproj_all, weight[0])
    gin_out[0] = (dnormed / rms_s[...]).astype(BF16)

    EH = EY // 2

    def w_part(r, h):
        rows = pl.ds(pl.multiple_of(((y + r) % NY) * EY + h * EH, EH), EH)
        return local[rows, mine_l] + c_recv[r, pl.ds(h * EH, EH), :].astype(F32)

    arrived(c_recv.at[2], c_sem.at[2])
    for way in (0, 1):
        wy_send[way, 2] = w_part(2, way).astype(BF16)
        send(wy_send.at[way, 2], wy_r1.at[way], wy1_sem.at[way], yn[way])
    for way, r in ((0, 1), (1, 3)):
        arrived(c_recv.at[r], c_sem.at[r])
        wy_send[way, 1 - way] = w_part(r, 1 - way).astype(BF16)
        send(wy_send.at[way, 1 - way], wy_r2.at[way, 1 - way], wy2_sem.at[way, 1 - way], yn[way])
    for way, r in ((0, 1), (1, 3)):
        arrived(wy_r1.at[way], wy1_sem.at[way])
        wy_send[way, way] = (w_part(r, way) + wy_r1[way].astype(F32)).astype(BF16)
        send(wy_send.at[way, way], wy_r2.at[way, way], wy2_sem.at[way, way], yn[way])
    arrived(c_recv.at[0], c_sem.at[0])
    total = []
    for h in (0, 1):
        value = w_part(0, h)
        for way in (0, 1):
            arrived(wy_r2.at[way, h], wy2_sem.at[way, h])
            value = value + wy_r2[way, h].astype(F32)
        total.append(value.astype(BF16))
    total = jnp.concatenate(total, axis=0)
    out_row = lax.broadcasted_iota(jnp.int32, (NZ * 48, EY), 0)
    in_row = lax.broadcasted_iota(jnp.int32, (NZ * 48, EY), 1)
    group = out_row // 24
    inner = out_row - group * 24
    spread = jnp.where(jnp.logical_and(inner < 18, in_row == group * 18 + inner), 1.0, 0.0).astype(BF16)
    wz_send[...] = dot(spread, total).astype(BF16).reshape(NZ, 48, LANES)
    for d in range(1, NZ):
        send(wz_send.at[(z + d) % NZ], wz_recv.at[d], wz_sem.at[d], zs[d])
    value = wz_send[z].astype(F32)
    for d in range(1, NZ):
        arrived(wz_recv.at[d], wz_sem.at[d])
        value = value + wz_recv[d].astype(F32)
    wc_send[...] = value.reshape(2, 24, LANES)
    send(wc_send.at[1 - c], wc_recv, wc_sem, sib)
    gw_out[0, :, mine_l] = wc_send[c, :18, :]
    arrived(wc_recv, wc_sem)
    gw_out[0, :, theirs_l] = wc_recv[:18, :]

    for cond, step in sent:
        if cond is None:
            step.wait_send()
        else:
            pl.when(cond)(step.wait_send)


def scratch():
    vmem, dma = pltpu.VMEM, pltpu.SemaphoreType.DMA
    return [
        vmem((ROWS, DH), BF16), vmem((ROWS, 1), F32), vmem((2, HALF, E), BF16), vmem((2, HALF, E), BF16),
        vmem((OWN, E), F32), vmem((OWN, E), F32), vmem((OWN, 1), F32), vmem((2, QUARTER, E), BF16),
        vmem((NZ, 2, 2, QUARTER, E), BF16), vmem((NY, 2, 2, HALF, E), BF16),
        vmem((NZ * OWN, E), F32), vmem((NY, 2, 2, HALF, E), BF16),
        vmem((NZ, HALF, E), BF16), vmem((NZ, HALF, E), BF16),
        vmem((2, 4, 2, QUARTER, E), BF16), vmem((2, 4, 2, QUARTER, E), BF16),
        vmem((2, 2, HALF, E), BF16), vmem((2, 2, 2, HALF, E), BF16),
        vmem((2, 2, HALF, E), BF16), vmem((2, HALF, E), BF16), vmem((2, HALF, E), BF16),
        vmem((2, QUARTER, E), BF16), vmem((2, QUARTER, E), BF16),
        vmem((OWN, E), F32), vmem((2, OWN, E), BF16),
        vmem((E, DH), F32), vmem((NY, EY, LANES), BF16), vmem((NY, EY, LANES), BF16),
        vmem((2, 3, EY // 2, LANES), BF16), vmem((2, EY // 2, LANES), BF16), vmem((2, 2, EY // 2, LANES), BF16),
        vmem((NZ, 48, LANES), BF16), vmem((NZ, 48, LANES), BF16),
        vmem((2, 24, LANES), F32), vmem((24, LANES), F32),
        dma((2, 2)), dma((2,)), dma((4, 2, 2, 2)), dma((NZ, 2, 2)), dma((2, 2, 2)), dma((2, 2, 2, 2)),
        dma((2, 2, 2)),
        dma((NZ, 2)), dma((2, 4, 2, 2)), dma((2, 2, 2)), dma((2, 2, 2, 2)), dma((2, 2)), dma((2, 2)),
        dma((2, 2)), dma((2,)),
        dma((NY, 2)), dma((2, 2)), dma((2, 2, 2)), dma((NZ, 2)), dma((2,)),
    ]


def shards(inputs, head_weight, pair_index):
    space = pl.BlockSpec(memory_space=pltpu.VMEM)
    return pl.pallas_call(
        kernel,
        out_shape=(
            jax.ShapeDtypeStruct((1, E // 64, DH), F32),
            jax.ShapeDtypeStruct((1, ROWS, DH), BF16),
        ),
        in_specs=[space] * 3,
        out_specs=(space, space),
        scratch_shapes=scratch(),
        compiler_params=pltpu.CompilerParams(
            collective_id=0, has_side_effects=True, vmem_limit_bytes=60 * 2**20
        ),
    )(inputs, head_weight, pair_index.reshape(ROWS, 1))


def solution(mesh):
    in_specs = (P("tower", "dp", None), P("tower", None, "mp"), P("dp"))
    out_specs = (P("tower", "dp", "mp"), P("tower", "dp", "mp"))
    return jax.shard_map(shards, mesh=mesh, in_specs=in_specs, out_specs=out_specs, check_vma=False)
```

time: 1080 us -> 125 us (0.12)
  waiting for transfers between devices: 688 us -> 0 us
  blocking collectives: 148 us -> 0 us
  matrix products: 124 us -> 0 us
  Pallas kernels: 0 us -> 120 us
  starting transfers between devices: 68.3 us -> 0 us
  between operations: 15.2 us -> 0.64 us
  local copies, waits for them, and re-layouts: 19.3 us -> 4.8 us
    ppermute x64 -> x0, waiting for transfers between devices: 590 us -> none  [the longest x63 581 us: from_behind(): return lax.ppermute(block, axis, route)]
    unnamed x1 -> x0, blocking collectives: 148 us -> none
    dot_general x67 -> x0, matrix products: 124 us -> none  [the longest x64 118 us: pair_grad(): return jnp.dot(coeffs, visitor, preferred_element_type=jnp.float32)]
    pallas_call x0 -> x1, Pallas kernels: none -> 120 us  [shards(): pl.pallas_call(kernel, out_shape=(jax.ShapeDtypeStruct((1, E // 64, DH),...]
    psum x2 -> x0, waiting for transfers between devices: 98.5 us -> none  [the longest x1 55.5 us: shards(): projected = lax.psum(partial_value, 'mp')]
    unnamed x16 -> x0, starting transfers between devices: 54.7 us -> none
    unnamed x40 -> x1, local copies, waits for them, and re-layouts: 15.6 us -> 1.77 us
    ppermute x64 -> x0, starting transfers between devices: 13.5 us -> none  [the longest x63 12.9 us: from_behind(): return lax.ppermute(block, axis, route)]
  transfers between devices with their start and end apart: 82 -> 0, of which waited for: 66 -> 0; matrix products, arithmetic and copies ran while one was open for 0% -> 0% of each run, Pallas kernels for 0% -> 0%
where the time goes in v1:
time: 125 us
  Pallas kernels  120 us (96%)
  local copies, waits for them, and re-layouts  4.8 us (4%)
    pallas_call x1, Pallas kernels, shards(): pl.pallas_call(kernel, out_shape=(jax.ShapeDtypeStruct((1, E // 64, DH),...  120 us

profile of v1, /device:TPU:5, one launch (start us, length us, event | category | flops | bytes accessed | tf_op | source)
XLA Modules:
  0.0 125.2 jit_solution(3565037292877284664)
XLA Ops:
  0.6 1.5 %copy.6.pairs = s32[256,1]{1,0:T(8,128)} copy(s32[256,1]{0,1:T(1,128)} %bitcast.1) | data formatting | bytes 2048 | tf_op jit(solution)/shard_map/reshape | solution.py:431
  2.1 119.7 %shard_map.50 = (f32[1,18,768]{2,1,0:T(8,128)}, bf16[1,256,768]{2,1,0:T(8,128)(2,1)}) custom-call(bf16[1,256,1536]{2,1,0:T(8,128)(2,1)} %pooled.1, bf16[1,1152,768]{2,1,0:T(8,128)(2,1)} %weight.1, s32[256,1]{1,0:T(8,128)} %copy.6.pairs), custom_call_target="tpu_custom_call" | custom-call | tf_op jit(solution)/shard_map/pallas_call | solution.py:419
  121.9 1.6 %copy.7 = f32[1,18,768]{2,0,1:T(1,128)} copy(f32[1,18,768]{2,1,0:T(8,128)} %get-tuple-element.4) | data formatting | bytes 110592 | tf_op jit(solution)/shard_map/pallas_call | solution.py:419
  123.4 1.8 %copy.9 = bf16[1,256,768]{2,1,0:T(8,128)(2,1)} copy(bf16[1,256,768]{2,1,0:T(8,128)(2,1)} %get-tuple-element.9) | data formatting | bytes 786432

commit v2 on v1

v2 whole, which is shorter than its diff:
```python
import jax
import jax.numpy as jnp
from jax import lax
from jax.experimental import pallas as pl
from jax.experimental.pallas import tpu as pltpu
from jax.sharding import PartitionSpec as P

EPSILON = 1e-06
LOGIT_SCALE = 100.0
LOGIT_BIAS = -10.0
BATCH = 16384
LOSS_SCALE = 16384.0
WEIGHT_PAIR = LOSS_SCALE * LOGIT_SCALE / BATCH
LOG2E = 1.4426950408889634
MAX_POWER = 126.0
NX, NY, NZ = 4, 4, 8
ROWS = 256
OWN = 128
HALF = 64
QUARTER = 32
E = 1152
D = 1536
DH = 768
LANES = 128
POS = (0, 1, 3, 5, 7, 6, 4, 2)
EY = 288
F32 = jnp.float32
BF16 = jnp.bfloat16
MESH = pl.DeviceIdType.MESH
NT = (((1,), (1,)), ((), ()))
TN = (((0,), (0,)), ((), ()))


def dot(a, b, dims=(((1,), (0,)), ((), ()))):
    return lax.dot_general(a, b, dims, preferred_element_type=F32)


def kernel(
    pooled, weight, pairs, gw_out, gin_out,
    normed, rms_s, hsend, hrecv, proj, unit, inv_s, ebuf,
    img, txt, igrad, tgrad, tacc, town,
    sib_send, sib_recv, zsend, zrecv, yr1, yr2, xsend, xl_recv, xr_recv, ib_send, ib_recv,
    grad, dfull,
    local, c_send, c_recv, wy_send, wy_r1, wy_r2, wz_send, wz_recv, wc_send, wc_recv,
    h_sem, ix_sem, zr_sem, sb_sem, tx_sem, ty_sem, tf_sem,
    rsb_sem, rz_sem, ry1_sem, ry2_sem, rx_sem, rr_sem, ib_sem, dx_sem,
    c_sem, wy1_sem, wy2_sem, wz_sem, wc_sem,
):
    dp = lax.axis_index("dp")
    tower = lax.axis_index("tower")
    mp = lax.axis_index("mp")
    x = tower * 2 + mp
    y = dp // 16
    z = (dp // 2) % 8
    c = dp % 2

    def at(nx, ny, nz, nc):
        return {"dp": (ny * NZ + nz) * 2 + nc, "tower": nx // 2, "mp": nx % 2}

    xl = at(tower * 2 + 1 - mp, y, z, c)
    xr = at(3 - x, y, z, c)
    sib = at(x, y, z, 1 - c)
    yn = (at(x, (y + 1) % NY, z, c), at(x, (y + NY - 1) % NY, z, c))
    zs = [at(x, y, (z + d) % NZ, c) for d in range(NZ)]
    zn = (zs[1], zs[NZ - 1])
    is_home = x >= 2
    is_image = x < 2
    first = jnp.where(is_home, x - 2, 1 - x)
    second = 1 - first
    order = (first, second)

    peers = [xl, xr, sib, yn[0], yn[1]] + zs[1:]
    barrier = pltpu.get_barrier_semaphore()
    for peer in peers:
        pl.semaphore_signal(barrier, inc=1, device_id=peer, device_id_type=MESH)

    sent = []

    def copy(src, dst, sem, device):
        return pltpu.make_async_remote_copy(
            src_ref=src, dst_ref=dst, send_sem=sem.at[0], recv_sem=sem.at[1],
            device_id=device, device_id_type=MESH,
        )

    def send(src, dst, sem, device):
        step = copy(src, dst, sem, device)
        step.start()
        sent.append((None, step))

    def send_if(cond, src, dst, sem, device):
        step = copy(src, dst, sem, device)
        pl.when(cond)(step.start)
        sent.append((cond, step))

    def arrived(dst, sem):
        copy(dst, dst, sem, sib).wait_recv()

    full = pooled[0].astype(F32)
    rms = jnp.sqrt(jnp.mean(full * full, axis=-1, keepdims=True) + EPSILON)
    rms_s[...] = rms
    part = pooled[0, :, pl.ds(pl.multiple_of(mp * DH, DH), DH)].astype(F32)
    normed[...] = (part / rms).astype(BF16)
    theirs = pl.ds(pl.multiple_of((1 - mp) * OWN, OWN), OWN)
    mine = pl.ds(pl.multiple_of(mp * OWN, OWN), OWN)
    hsend[...] = dot(normed[theirs, :], weight[0], NT).astype(BF16).reshape(2, HALF, E)
    pl.semaphore_wait(barrier, len(peers))
    for j in (1, 0):
        send(hsend.at[j], hrecv.at[j], h_sem.at[j], xl)
    proj[...] = dot(normed[mine, :], weight[0], NT)

    def text_first(j):
        steps = [copy(txt.at[0, first, j], txt.at[0, first, j], tx_sem.at[j, 1], xl)]
        for way, slot in ((0, 3), (1, 1)):
            steps.append(copy(txt.at[0, first, j], txt.at[slot, first, j], ty_sem.at[0, j, way], yn[way]))
        return steps

    def own_image():
        for ch in (0, 1):
            for way in (0, 1):
                to = POS[NZ - 1] if way == 0 else POS[1]
                steps = copy(img.at[0, 0, ch], img.at[to, 0, ch], zr_sem.at[0, way, ch], zn[way])
                steps.start()
            copy(img.at[0, 0, ch], img.at[0, 1, ch], sb_sem.at[0, ch], sib).start()

    for j in (1, 0):
        arrived(hrecv.at[j], h_sem.at[j])
        rows = pl.ds(j * HALF, HALF)
        value = proj[rows, :] + hrecv[j].astype(F32)
        inverse = lax.rsqrt(jnp.sum(value * value, axis=-1, keepdims=True) + EPSILON)
        inv_s[rows, :] = inverse
        unit_j = value * inverse
        unit[rows, :] = unit_j
        embedded = unit_j.astype(BF16)

        @pl.when(is_home)
        def _():
            txt[0, first, j] = embedded
            copy(txt.at[0, first, j], txt.at[0, first, j], tx_sem.at[j, 0], xr).start()
            for step in text_first(j):
                step.start()

        @pl.when(is_image)
        def _():
            if j == 0:
                img[0, 0] = embedded.reshape(2, QUARTER, E)
                own_image()
            else:
                ebuf[...] = embedded.reshape(2, QUARTER, E)
                copy(ebuf, img.at[0, 0], ix_sem, xr).start()

        sent.append((is_home, copy(txt.at[0, first, j], txt.at[0, first, j], tx_sem.at[j, 0], xr)))
        sent.extend((None, step) for step in text_first(j))
    sent.append((is_image, copy(ebuf, img.at[0, 0], ix_sem, xr)))
    for ch in (0, 1):
        for way in (0, 1):
            to = POS[NZ - 1] if way == 0 else POS[1]
            sent.append((None, copy(img.at[0, 0, ch], img.at[to, 0, ch], zr_sem.at[0, way, ch], zn[way])))
        sent.append((None, copy(img.at[0, 0, ch], img.at[0, 1, ch], sb_sem.at[0, ch], sib)))

    @pl.when(is_home)
    def _():
        arrived(img.at[0, 0], ix_sem)
        own_image()

    @pl.when(is_image)
    def _():
        for j in (1, 0):
            arrived(txt.at[0, first, j], tx_sem.at[j, 0])
            for step in text_first(j):
                step.start()

    def ring_arrive(k):
        for ch in (0, 1):
            for way in (0, 1):
                if k == 4 and ch != way:
                    continue
                slot = (NZ - k) % NZ if way == 0 else k
                p = POS[slot]
                arrived(img.at[p, 0, ch], zr_sem.at[k - 1, way, ch])
                if k < 4 and not (k == 3 and ch != way):
                    to = POS[(slot - 1) % NZ if way == 0 else (slot + 1) % NZ]
                    send(img.at[p, 0, ch], img.at[to, 0, ch], zr_sem.at[k, way, ch], zn[way])
                send(img.at[p, 0, ch], img.at[p, 1, ch], sb_sem.at[p, ch], sib)

    def y_forward(a):
        xs = order[a]
        for way, slot in ((0, 3), (1, 1)):
            for j in (1, 0):
                arrived(txt.at[slot, xs, j], ty_sem.at[a, j, way])
                if j == way:
                    send(txt.at[slot, xs, j], txt.at[2, xs, j], tf_sem.at[a, j], yn[way])

    def sibling_images(low, high):
        for p in range(low, high):
            for ch in (0, 1):
                arrived(img.at[p, 1, ch], sb_sem.at[p, ch])

    mp_source = jnp.where(is_image, x, 3 - x)
    offset = jnp.where(is_image, 0, HALF)
    row = (pairs[pl.ds(mp_source, 1), :] - dp * ROWS).astype(F32)
    lane = lax.broadcasted_iota(jnp.int32, (HALF, OWN), 1)
    down = lax.broadcasted_iota(jnp.int32, (HALF, OWN), 0) + offset
    positions = jnp.sum(jnp.where(lane == down, row, 0.0), axis=1, keepdims=True)

    def block(t, low, high, masked=False):
        count = (high - low) * OWN
        images = img[low:high].reshape(count, E)
        texts = txt[t].reshape(ROWS, E)
        power = dot(images, texts, NT) * (-LOGIT_SCALE * LOG2E) - LOGIT_BIAS * LOG2E
        if masked:
            columns = lax.broadcasted_iota(jnp.int32, (HALF, ROWS), 1).astype(F32)
            sign = jnp.where(positions == columns, -1.0, 1.0)
            top = WEIGHT_PAIR * sign / (1.0 + jnp.exp2(jnp.minimum(sign * power[:HALF], MAX_POWER)))
            rest = WEIGHT_PAIR / (1.0 + jnp.exp2(jnp.minimum(power[HALF:], MAX_POWER)))
            coeffs = jnp.concatenate([top, rest], axis=0).astype(BF16)
        else:
            coeffs = (WEIGHT_PAIR / (1.0 + jnp.exp2(jnp.minimum(power, MAX_POWER)))).astype(BF16)
        rows = pl.ds(low * OWN, count)
        for_images = dot(coeffs, texts)
        if t == 0:
            igrad[rows, :] = for_images
        else:
            igrad[rows, :] += for_images
        return dot(coeffs, images, TN)

    ring_arrive(1)
    for j in (1, 0):
        arrived(txt.at[0, second, j], tx_sem.at[j, 1])
        for way, slot in ((0, 3), (1, 1)):
            send(txt.at[0, second, j], txt.at[slot, second, j], ty_sem.at[1, j, way], yn[way])
    sibling_images(0, 1)
    town[...] = block(0, 0, 1, masked=True)
    ring_arrive(2)
    y_forward(0)
    sibling_images(1, 3)
    town[...] += block(0, 1, 3)
    ring_arrive(3)
    sibling_images(3, 5)
    town[...] += block(0, 3, 5)
    y_forward(1)
    ring_arrive(4)
    sibling_images(5, 7)
    town[...] += block(0, 5, 7)
    sibling_images(7, 8)
    town[...] += block(0, 7, 8)

    for way, slot in ((0, 1), (1, 3)):
        tgrad[slot] = block(slot, 0, NZ).astype(BF16).reshape(2, 2, HALF, E)
        for a in (1, 0):
            send(tgrad.at[slot, order[a], 1 - way], yr2.at[a, way, 1 - way], ry2_sem.at[a, way, 1 - way], yn[way])

    for a in (0, 1):
        for j in (0, 1):
            arrived(txt.at[2, order[a], j], tf_sem.at[a, j])

    def sibling_rows(slot):
        p = POS[slot]
        sib_send[p] = igrad[pl.ds(p * OWN + HALF, HALF), :].astype(BF16)
        send(sib_send.at[p], sib_recv.at[p], rsb_sem.at[p], sib)

    def z_send(way, far, ch):
        slot = far if way == 0 else NZ - far
        p = POS[slot]
        rows = pl.ds(p * OWN + ch * QUARTER, QUARTER)
        value = igrad[rows, :] + sib_recv[p, pl.ds(ch * QUARTER, QUARTER), :].astype(F32)
        if far < 3 or (far == 3 and ch == way):
            arrived(zrecv.at[way, far, ch], rz_sem.at[way, far, ch])
            value = value + zrecv[way, far, ch].astype(F32)
        zsend[way, far - 1, ch] = value.astype(BF16)
        send(zsend.at[way, far - 1, ch], zrecv.at[way, far - 1, ch], rz_sem.at[way, far - 1, ch], zn[way])

    def sibling_here(*slots):
        for slot in slots:
            arrived(sib_recv.at[POS[slot]], rsb_sem.at[POS[slot]])

    tacc[...] = block(2, 7, 8)
    sibling_rows(4)
    tacc[...] += block(2, 5, 7)
    sibling_rows(3)
    sibling_rows(5)
    sibling_here(4)
    for way in (0, 1):
        z_send(way, 4, way)
    tacc[...] += block(2, 3, 5)
    sibling_rows(2)
    sibling_rows(6)
    sibling_here(3, 5)
    for way in (0, 1):
        z_send(way, 3, 1 - way)
    tacc[...] += block(2, 1, 3)
    sibling_rows(1)
    sibling_rows(7)
    tgrad[2] = (tacc[...] + block(2, 0, 1)).astype(BF16).reshape(2, 2, HALF, E)
    sibling_rows(0)

    for a in (1, 0):
        for way in (0, 1):
            send(tgrad.at[2, order[a], way], yr1.at[a, way], ry1_sem.at[a, way], yn[way])
    for way in (0, 1):
        z_send(way, 3, way)

    def y_second(a):
        xs = order[a]
        for way, slot in ((0, 1), (1, 3)):
            arrived(yr1.at[a, way], ry1_sem.at[a, way])
            tgrad[slot, xs, way] = (tgrad[slot, xs, way].astype(F32) + yr1[a, way].astype(F32)).astype(BF16)
            send(tgrad.at[slot, xs, way], yr2.at[a, way, way], ry2_sem.at[a, way, way], yn[way])

    sibling_here(2, 6, 1, 7, 0)
    for way in (0, 1):
        z_send(way, 2, 1 - way)
    y_second(1)
    for way in (0, 1):
        z_send(way, 2, way)
    y_second(0)
    for way in (0, 1):
        z_send(way, 1, 1 - way)
    for way in (0, 1):
        z_send(way, 1, way)

    def y_total(a, j):
        for way in (0, 1):
            arrived(yr2.at[a, way, j], ry2_sem.at[a, way, j])
        rows = pl.ds(pl.multiple_of(order[a] * OWN + j * HALF, HALF), HALF)
        return town[rows, :] + yr2[a, 0, j].astype(F32) + yr2[a, 1, j].astype(F32)

    for j in (0, 1):
        xsend[1, j] = y_total(1, j).astype(BF16)
        send(xsend.at[1, j], xl_recv.at[j], rx_sem.at[j], xl)

    for ch in (0, 1):
        rows = pl.ds(ch * QUARTER, QUARTER)
        value = igrad[rows, :] + sib_recv[0, rows, :].astype(F32)
        for way in (0, 1):
            arrived(zrecv.at[way, 0, ch], rz_sem.at[way, 0, ch])
            value = value + zrecv[way, 0, ch].astype(F32)

        @pl.when(is_image)
        def _():
            grad[rows, :] = value

        @pl.when(is_home)
        def _():
            ib_send[ch] = value.astype(BF16)

        send_if(is_home, ib_send.at[ch], ib_recv.at[ch], ib_sem.at[ch], xr)

    def dx_copy(j):
        part = pl.ds(j * HALF, HALF)
        return copy(dfull.at[mp, part], dfull.at[mp, part], dx_sem.at[j], xl)

    def backward(j):
        part = pl.ds(j * HALF, HALF)
        unit_v = unit[part, :]
        grad_v = grad[part, :]
        dproj = (grad_v - unit_v * jnp.sum(unit_v * grad_v, axis=-1, keepdims=True)) * inv_s[part, :]
        dfull[mp, part] = dproj.astype(BF16)
        dx_copy(j).start()

    pl.when(is_image)(lambda: backward(0))

    for j in (0, 1):
        value = y_total(0, j)
        arrived(xl_recv.at[j], rx_sem.at[j])
        value = value + xl_recv[j].astype(F32)

        @pl.when(is_image)
        def _():
            xsend[0, j] = value.astype(BF16)

        send_if(is_image, xsend.at[0, j], xr_recv.at[j], rr_sem.at[j], xr)

        @pl.when(is_home)
        def _():
            grad[pl.ds(j * HALF, HALF), :] = value

    @pl.when(is_image)
    def _():
        for ch in (0, 1):
            arrived(ib_recv.at[ch], ib_sem.at[ch])
        grad[pl.ds(HALF, HALF), :] = ib_recv[...].astype(F32).reshape(HALF, E)
        backward(1)

    @pl.when(is_home)
    def _():
        for j in (0, 1):
            arrived(xr_recv.at[j], rr_sem.at[j])
            rows = pl.ds(j * HALF, HALF)
            grad[rows, :] = grad[rows, :] + xr_recv[j].astype(F32)
            backward(j)

    for j in (0, 1):
        sent.append((None, dx_copy(j)))
    for j in (0, 1):
        part = pl.ds(j * HALF, HALF)
        arrived(dfull.at[1 - mp, part], dx_sem.at[j])
    dproj_all = dfull[...].reshape(ROWS, E)

    theirs_l = pl.ds(pl.multiple_of((1 - c) * LANES, LANES), LANES)
    mine_l = pl.ds(pl.multiple_of(c * LANES, LANES), LANES)
    for l in range(3):
        local[l] = dot(dproj_all, normed[:, l * 2 * LANES:(l + 1) * 2 * LANES], TN)
        c_send[l] = local[l, :, theirs_l].astype(BF16)
        send(c_send.at[l], c_recv.at[l], c_sem.at[l], sib)

    dnormed = dot(dproj_all, weight[0])
    gin_out[0] = (dnormed / rms_s[...]).astype(BF16)

    EH = EY // 2

    def w_part(l, r, h):
        rows = pl.ds(pl.multiple_of(((y + r) % NY) * EY + h * EH, EH), EH)
        return local[l, rows, mine_l] + c_recv[l, rows, :].astype(F32)

    for l in range(3):
        arrived(c_recv.at[l], c_sem.at[l])
        for way in (0, 1):
            wy_send[l, way, 2] = w_part(l, 2, way).astype(BF16)
            send(wy_send.at[l, way, 2], wy_r1.at[l, way], wy1_sem.at[l, way], yn[way])
        for way, r in ((0, 1), (1, 3)):
            wy_send[l, way, 1 - way] = w_part(l, r, 1 - way).astype(BF16)
            send(wy_send.at[l, way, 1 - way], wy_r2.at[l, way, 1 - way], wy2_sem.at[l, way, 1 - way], yn[way])
    for l in range(3):
        for way, r in ((0, 1), (1, 3)):
            arrived(wy_r1.at[l, way], wy1_sem.at[l, way])
            wy_send[l, way, way] = (w_part(l, r, way) + wy_r1[l, way].astype(F32)).astype(BF16)
            send(wy_send.at[l, way, way], wy_r2.at[l, way, way], wy2_sem.at[l, way, way], yn[way])
    out_row = lax.broadcasted_iota(jnp.int32, (NZ * 48, EY), 0)
    in_row = lax.broadcasted_iota(jnp.int32, (NZ * 48, EY), 1)
    group = out_row // 24
    inner = out_row - group * 24
    spread = jnp.where(jnp.logical_and(inner < 18, in_row == group * 18 + inner), 1.0, 0.0).astype(BF16)
    for l in range(3):
        total = []
        for h in (0, 1):
            value = w_part(l, 0, h)
            for way in (0, 1):
                arrived(wy_r2.at[l, way, h], wy2_sem.at[l, way, h])
                value = value + wy_r2[l, way, h].astype(F32)
            total.append(value.astype(BF16))
        total = jnp.concatenate(total, axis=0)
        wz_send[l] = dot(spread, total).astype(BF16).reshape(NZ, 48, LANES)
        for d in range(1, NZ):
            send(wz_send.at[l, (z + d) % NZ], wz_recv.at[l, d], wz_sem.at[l, d], zs[d])
    for l in range(3):
        value = wz_send[l, z].astype(F32)
        for d in range(1, NZ):
            arrived(wz_recv.at[l, d], wz_sem.at[l, d])
            value = value + wz_recv[l, d].astype(F32)
        wc_send[l] = value.reshape(2, 24, LANES)
        send(wc_send.at[l, 1 - c], wc_recv.at[l], wc_sem.at[l], sib)
        gw_out[0, :, pl.ds(pl.multiple_of((2 * l + c) * LANES, LANES), LANES)] = wc_send[l, c, :18, :]
    for l in range(3):
        arrived(wc_recv.at[l], wc_sem.at[l])
        gw_out[0, :, pl.ds(pl.multiple_of((2 * l + 1 - c) * LANES, LANES), LANES)] = wc_recv[l, :18, :]

    for cond, step in sent:
        if cond is None:
            step.wait_send()
        else:
            pl.when(cond)(step.wait_send)


def scratch():
    vmem, dma = pltpu.VMEM, pltpu.SemaphoreType.DMA
    return [
        vmem((ROWS, DH), BF16), vmem((ROWS, 1), F32), vmem((2, HALF, E), BF16), vmem((2, HALF, E), BF16),
        vmem((OWN, E), F32), vmem((OWN, E), F32), vmem((OWN, 1), F32), vmem((2, QUARTER, E), BF16),
        vmem((NZ, 2, 2, QUARTER, E), BF16), vmem((NY, 2, 2, HALF, E), BF16),
        vmem((NZ * OWN, E), F32), vmem((NY, 2, 2, HALF, E), BF16), vmem((ROWS, E), F32), vmem((ROWS, E), F32),
        vmem((NZ, HALF, E), BF16), vmem((NZ, HALF, E), BF16),
        vmem((2, 4, 2, QUARTER, E), BF16), vmem((2, 4, 2, QUARTER, E), BF16),
        vmem((2, 2, HALF, E), BF16), vmem((2, 2, 2, HALF, E), BF16),
        vmem((2, 2, HALF, E), BF16), vmem((2, HALF, E), BF16), vmem((2, HALF, E), BF16),
        vmem((2, QUARTER, E), BF16), vmem((2, QUARTER, E), BF16),
        vmem((OWN, E), F32), vmem((2, OWN, E), BF16),
        vmem((3, E, 2 * LANES), F32), vmem((3, E, LANES), BF16), vmem((3, E, LANES), BF16),
        vmem((3, 2, 3, EY // 2, LANES), BF16), vmem((3, 2, EY // 2, LANES), BF16), vmem((3, 2, 2, EY // 2, LANES), BF16),
        vmem((3, NZ, 48, LANES), BF16), vmem((3, NZ, 48, LANES), BF16),
        vmem((3, 2, 24, LANES), F32), vmem((3, 24, LANES), F32),
        dma((2, 2)), dma((2,)), dma((4, 2, 2, 2)), dma((NZ, 2, 2)), dma((2, 2, 2)), dma((2, 2, 2, 2)),
        dma((2, 2, 2)),
        dma((NZ, 2)), dma((2, 4, 2, 2)), dma((2, 2, 2)), dma((2, 2, 2, 2)), dma((2, 2)), dma((2, 2)),
        dma((2, 2)), dma((2, 2)),
        dma((3, 2)), dma((3, 2, 2)), dma((3, 2, 2, 2)), dma((3, NZ, 2)), dma((3, 2)),
    ]


def shards(inputs, head_weight, pair_index):
    space = pl.BlockSpec(memory_space=pltpu.VMEM)
    return pl.pallas_call(
        kernel,
        out_shape=(
            jax.ShapeDtypeStruct((1, E // 64, DH), F32),
            jax.ShapeDtypeStruct((1, ROWS, DH), BF16),
        ),
        in_specs=[space] * 3,
        out_specs=(space, space),
        scratch_shapes=scratch(),
        compiler_params=pltpu.CompilerParams(
            collective_id=0, has_side_effects=True, vmem_limit_bytes=60 * 2**20
        ),
    )(inputs, head_weight, pair_index.reshape(2, OWN))


def solution(mesh):
    in_specs = (P("tower", "dp", None), P("tower", None, "mp"), P("dp"))
    out_specs = (P("tower", "dp", "mp"), P("tower", "dp", "mp"))
    return jax.shard_map(shards, mesh=mesh, in_specs=in_specs, out_specs=out_specs, check_vma=False)
```

time: 125 us -> 110 us (0.88)
  Pallas kernels: 120 us -> 106 us
  local copies, waits for them, and re-layouts: 4.8 us -> 3.33 us
    pallas_call x1, Pallas kernels: 120 us -> 106 us  [shards(): pl.pallas_call(kernel, out_shape=(jax.ShapeDtypeStruct((1, E // 64, DH),...]
    reshape x1 -> x0, local copies, waits for them, and re-layouts: 1.47 us -> none  [shards(): pair_index.reshape(ROWS, 1)]
where the time goes in v2:
time: 110 us
  Pallas kernels  106 us (96%)
  local copies, waits for them, and re-layouts  3.33 us (3%)
    pallas_call x1, Pallas kernels, shards(): pl.pallas_call(kernel, out_shape=(jax.ShapeDtypeStruct((1, E // 64, DH),...  106 us

profile of v2, /device:TPU:5, one launch (start us, length us, event | category | flops | bytes accessed | tf_op | source)
XLA Modules:
  0.0 110.2 jit_solution(15438411078247195178)
XLA Ops:
  0.6 106.2 %shard_map.50 = (f32[1,18,768]{2,1,0:T(8,128)}, bf16[1,256,768]{2,1,0:T(8,128)(2,1)}) custom-call(bf16[1,256,1536]{2,1,0:T(8,128)(2,1)} %pooled.1, bf16[1,1152,768]{2,1,0:T(8,128)(2,1)} %weight.1, s32[2,128]{1,0:T(2,128)} %bitcast.1), custom_call_target="tpu_custom_call" | custom-call | tf_op jit(solution)/shard_map/pallas_call | solution.py:491
  106.9 1.6 %copy.5 = f32[1,18,768]{2,0,1:T(1,128)} copy(f32[1,18,768]{2,1,0:T(8,128)} %get-tuple-element.2) | data formatting | bytes 110592 | tf_op jit(solution)/shard_map/pallas_call | solution.py:491
  108.4 1.8 %copy.7 = bf16[1,256,768]{2,1,0:T(8,128)(2,1)} copy(bf16[1,256,768]{2,1,0:T(8,128)(2,1)} %get-tuple-element.7) | data formatting | bytes 786432

commit v3 on v2

v3 whole, which is shorter than its diff:
```python
import jax
import jax.numpy as jnp
from jax import lax
from jax.experimental import pallas as pl
from jax.experimental.pallas import tpu as pltpu
from jax.sharding import PartitionSpec as P

EPSILON = 1e-06
LOGIT_SCALE = 100.0
LOGIT_BIAS = -10.0
BATCH = 16384
LOSS_SCALE = 16384.0
WEIGHT_PAIR = LOSS_SCALE * LOGIT_SCALE / BATCH
LOG2E = 1.4426950408889634
MAX_POWER = 126.0
NX, NY, NZ = 4, 4, 8
ROWS = 256
OWN = 128
HALF = 64
QUARTER = 32
E = 1152
D = 1536
DH = 768
LANES = 128
POS = (0, 1, 3, 5, 7, 6, 4, 2)
EY = 288
TURN = (2, 3, 0, 1)
RTURN = (0, 2, 1, 3)
F32 = jnp.float32
BF16 = jnp.bfloat16
MESH = pl.DeviceIdType.MESH
NT = (((1,), (1,)), ((), ()))
TN = (((0,), (0,)), ((), ()))


def dot(a, b, dims=(((1,), (0,)), ((), ()))):
    return lax.dot_general(a, b, dims, preferred_element_type=F32)


def kernel(
    pooled, weight, pairs, gw_out, gin_out,
    normed, rms_s, hsend, hrecv, proj, unit, inv_s, ebuf,
    img, txt, igrad, tgrad, coef, town, beside,
    sib_send, sib_recv, zsend, zrecv, yr1, yr2, xsend, xl_recv, xr_recv, ib_send, ib_recv,
    grad, dfull,
    local, c_send, c_recv, wy_send, wy_r1, wy_r2, wz_send, wz_recv, wc_send, wc_recv,
    h_sem, ix_sem, zr_sem, sb_sem, tx_sem, ty_sem, tf_sem,
    rsb_sem, rz_sem, ry1_sem, ry2_sem, rx_sem, rr_sem, ib_sem, dx_sem,
    c_sem, wy1_sem, wy2_sem, wz_sem, wc_sem,
):
    dp = lax.axis_index("dp")
    tower = lax.axis_index("tower")
    mp = lax.axis_index("mp")
    x = tower * 2 + mp
    y = dp // 16
    z = (dp // 2) % 8
    c = dp % 2

    def at(nx, ny, nz, nc):
        return {"dp": (ny * NZ + nz) * 2 + nc, "tower": nx // 2, "mp": nx % 2}

    xl = at(tower * 2 + 1 - mp, y, z, c)
    xr = at(3 - x, y, z, c)
    sib = at(x, y, z, 1 - c)
    yn = (at(x, (y + 1) % NY, z, c), at(x, (y + NY - 1) % NY, z, c))
    zs = [at(x, y, (z + d) % NZ, c) for d in range(NZ)]
    zn = (zs[1], zs[NZ - 1])
    is_home = x >= 2
    is_image = x < 2
    first = jnp.where(is_home, x - 2, 1 - x)
    second = 1 - first
    order = (first, second)

    peers = [xl, xr, sib, yn[0], yn[1]] + zs[1:]
    barrier = pltpu.get_barrier_semaphore()
    for peer in peers:
        pl.semaphore_signal(barrier, inc=1, device_id=peer, device_id_type=MESH)

    sent = []
    mode = {"run": True, "keep": True}

    def copy(src, dst, sem, device):
        return pltpu.make_async_remote_copy(
            src_ref=src, dst_ref=dst, send_sem=sem.at[0], recv_sem=sem.at[1],
            device_id=device, device_id_type=MESH,
        )

    def send(src, dst, sem, device, cond=None):
        step = copy(src, dst, sem, device)
        if mode["run"]:
            step.start()
        if mode["keep"]:
            sent.append((cond, step))

    def send_if(cond, src, dst, sem, device):
        step = copy(src, dst, sem, device)
        pl.when(cond)(step.start)
        sent.append((cond, step))

    def arrived(dst, sem):
        if mode["run"]:
            copy(dst, dst, sem, sib).wait_recv()

    def settle(count):
        for cond, step in sent[:count]:
            if cond is None:
                step.wait_send()
            else:
                pl.when(cond)(step.wait_send)
        del sent[:count]

    def only(cond, work):
        mode["keep"] = False
        pl.when(cond)(work)
        mode["keep"] = True

    def keep(work):
        mode["run"] = False
        work()
        mode["run"] = True

    full = pooled[0].astype(F32)
    rms = jnp.sqrt(jnp.mean(full * full, axis=-1, keepdims=True) + EPSILON)
    rms_s[...] = rms
    part = pooled[0, :, pl.ds(pl.multiple_of(mp * DH, DH), DH)].astype(F32)
    normed[...] = (part / rms).astype(BF16)
    theirs = pl.ds(pl.multiple_of((1 - mp) * OWN, OWN), OWN)
    mine = pl.ds(pl.multiple_of(mp * OWN, OWN), OWN)
    hsend[...] = dot(normed[theirs, :], weight[0], NT).astype(BF16).reshape(4, QUARTER, E)
    pl.semaphore_wait(barrier, len(peers))
    for j in TURN:
        send(hsend.at[j], hrecv.at[j], h_sem.at[j], xl)
    proj[...] = dot(normed[mine, :], weight[0], NT)

    def y_both(a, j):
        xs = order[a]
        for way, slot in ((0, 3), (1, 1)):
            send(txt.at[0, xs, j], txt.at[slot, xs, j], ty_sem.at[a, j, way], yn[way])

    def first_on(j):
        send(txt.at[0, first, j], txt.at[0, first, j], tx_sem.at[j, 1], xl)
        y_both(0, j)

    def own_image(ch):
        for way in (0, 1):
            to = POS[NZ - 1] if way == 0 else POS[1]
            send(img.at[0, 0, ch], img.at[to, 0, ch], zr_sem.at[0, way, ch], zn[way])
        send(img.at[0, 0, ch], img.at[0, 1, ch], sb_sem.at[0, ch], sib)

    for j in TURN:
        arrived(hrecv.at[j], h_sem.at[j])
        rows = pl.ds(j * QUARTER, QUARTER)
        value = proj[rows, :] + hrecv[j].astype(F32)
        inverse = lax.rsqrt(jnp.sum(value * value, axis=-1, keepdims=True) + EPSILON)
        inv_s[rows, :] = inverse
        unit_j = value * inverse
        unit[rows, :] = unit_j
        embedded = unit_j.astype(BF16)

        def text_start():
            send(txt.at[0, first, j], txt.at[0, first, j], tx_sem.at[j, 0], xr, is_home)
            first_on(j)

        def image_start():
            if j >= 2:
                send(ebuf.at[j - 2], img.at[0, 0, j - 2], ix_sem.at[j - 2], xr, is_image)
            else:
                own_image(j)

        def text_all():
            txt[0, first, j] = embedded
            text_start()

        def image_all():
            if j >= 2:
                ebuf[j - 2] = embedded
            else:
                img[0, 0, j] = embedded
            image_start()

        only(is_home, text_all)
        only(is_image, image_all)
        keep(text_start)
        keep(image_start)

    def ring(k, ch):
        for way in (0, 1):
            if k == 4 and ch != way:
                continue
            slot = (NZ - k) % NZ if way == 0 else k
            p = POS[slot]
            arrived(img.at[p, 0, ch], zr_sem.at[k - 1, way, ch])
            if k < 4 and not (k == 3 and ch != way):
                to = POS[(slot - 1) % NZ if way == 0 else (slot + 1) % NZ]
                send(img.at[p, 0, ch], img.at[to, 0, ch], zr_sem.at[k, way, ch], zn[way])
            send(img.at[p, 0, ch], img.at[p, 1, ch], sb_sem.at[p, ch], sib)

    def y_forward(a, j):
        xs = order[a]
        for way, slot in ((0, 3), (1, 1)):
            arrived(txt.at[slot, xs, j], ty_sem.at[a, j, way])
            if j // 2 == way:
                send(txt.at[slot, xs, j], txt.at[2, xs, j], tf_sem.at[a, j], yn[way])

    def first_here(j):
        arrived(txt.at[0, first, j], tx_sem.at[j, 0])
        first_on(j)

    def second_on(j):
        arrived(txt.at[0, second, j], tx_sem.at[j, 1])
        y_both(1, j)

    def image_device():
        first_here(2)
        first_here(3)
        first_here(0)
        ring(1, 0)
        first_here(1)
        ring(1, 1)
        second_on(2)
        second_on(3)
        ring(2, 0)
        second_on(0)
        ring(2, 1)
        y_forward(0, 0)
        second_on(1)
        y_forward(0, 2)
        y_forward(0, 3)
        y_forward(0, 1)

    def text_device():
        for ch in (0, 1):
            arrived(img.at[0, 0, ch], ix_sem.at[ch])
            own_image(ch)
        both_devices()

    def both_devices():
        y_forward(0, 2)
        y_forward(0, 3)
        second_on(2)
        second_on(3)
        y_forward(0, 0)
        second_on(0)
        ring(1, 0)
        y_forward(0, 1)
        second_on(1)
        ring(1, 1)
        ring(2, 0)
        ring(2, 1)

    only(is_image, image_device)
    only(is_home, text_device)
    keep(both_devices)

    def sibling_images(low, high):
        for p in range(low, high):
            for ch in (0, 1):
                arrived(img.at[p, 1, ch], sb_sem.at[p, ch])

    mp_source = jnp.where(is_image, x, 3 - x)
    offset = jnp.where(is_image, 0, HALF)
    row = (pairs[pl.ds(mp_source, 1), :] - dp * ROWS).astype(F32)
    lane = lax.broadcasted_iota(jnp.int32, (HALF, OWN), 1)
    down = lax.broadcasted_iota(jnp.int32, (HALF, OWN), 0) + offset
    positions = jnp.sum(jnp.where(lane == down, row, 0.0), axis=1, keepdims=True)

    def block(t, low, high, masked=False):
        count = (high - low) * OWN
        images = img[low:high].reshape(count, E)
        texts = txt[t].reshape(ROWS, E)
        power = dot(images, texts, NT) * (-LOGIT_SCALE * LOG2E) - LOGIT_BIAS * LOG2E
        if masked:
            columns = lax.broadcasted_iota(jnp.int32, (HALF, ROWS), 1).astype(F32)
            sign = jnp.where(positions == columns, -1.0, 1.0)
            top = WEIGHT_PAIR * sign / (1.0 + jnp.exp2(jnp.minimum(sign * power[:HALF], MAX_POWER)))
            rest = WEIGHT_PAIR / (1.0 + jnp.exp2(jnp.minimum(power[HALF:], MAX_POWER)))
            coeffs = jnp.concatenate([top, rest], axis=0).astype(BF16)
        else:
            coeffs = (WEIGHT_PAIR / (1.0 + jnp.exp2(jnp.minimum(power, MAX_POWER)))).astype(BF16)
        coef[pl.ds(low * OWN, count), t * ROWS:(t + 1) * ROWS] = coeffs
        return dot(coeffs, images, TN)

    def image_block(low, high):
        rows = pl.ds(low * OWN, (high - low) * OWN)
        igrad[rows, :] = dot(coef[rows, :], txt[...].reshape(NY * ROWS, E))

    y_forward(1, 2)
    ring(3, 0)
    y_forward(1, 3)
    ring(3, 1)
    y_forward(1, 0)
    y_forward(1, 1)
    sibling_images(0, 5)
    town[...] = block(0, 0, 5, masked=True)
    ring(4, 0)
    beside[0] = block(1, 0, 5)
    ring(4, 1)
    beside[1] = block(3, 0, 5)
    sibling_images(5, 8)

    gathered = len(sent)

    for way, slot in ((0, 1), (1, 3)):
        tgrad[slot] = (beside[way] + block(slot, 5, 8)).astype(BF16).reshape(2, 4, QUARTER, E)
        for a in (1, 0):
            for j in (2 - 2 * way, 3 - 2 * way):
                send(tgrad.at[slot, order[a], j], yr2.at[a, way, j], ry2_sem.at[a, way, j], yn[way])

    for a in (0, 1):
        for j in range(4):
            arrived(txt.at[2, order[a], j], tf_sem.at[a, j])

    def sibling_rows(slot):
        p = POS[slot]
        sib_send[p] = igrad[pl.ds(p * OWN + HALF, HALF), :].astype(BF16)
        send(sib_send.at[p], sib_recv.at[p], rsb_sem.at[p], sib)

    def z_send(way, far, ch):
        slot = far if way == 0 else NZ - far
        p = POS[slot]
        rows = pl.ds(p * OWN + ch * QUARTER, QUARTER)
        value = igrad[rows, :] + sib_recv[p, pl.ds(ch * QUARTER, QUARTER), :].astype(F32)
        if far < 3 or (far == 3 and ch == way):
            arrived(zrecv.at[way, far, ch], rz_sem.at[way, far, ch])
            value = value + zrecv[way, far, ch].astype(F32)
        zsend[way, far - 1, ch] = value.astype(BF16)
        send(zsend.at[way, far - 1, ch], zrecv.at[way, far - 1, ch], rz_sem.at[way, far - 1, ch], zn[way])

    def sibling_here(*slots):
        for slot in slots:
            arrived(sib_recv.at[POS[slot]], rsb_sem.at[POS[slot]])

    tgrad[2] = block(2, 0, NZ).astype(BF16).reshape(2, 4, QUARTER, E)
    for a in (1, 0):
        for i in (0, 1):
            for way in (0, 1):
                j = 2 * way + i
                send(tgrad.at[2, order[a], j], yr1.at[a, j], ry1_sem.at[a, j], yn[way])

    town[...] += block(0, 5, 8)
    image_block(5, 8)
    for slot in (4, 3, 5):
        sibling_rows(slot)
    image_block(3, 5)
    for slot in (2, 6):
        sibling_rows(slot)
    sibling_here(4, 3, 5)
    for way in (0, 1):
        z_send(way, 4, way)
    for way in (0, 1):
        z_send(way, 3, 1 - way)
    image_block(0, 3)
    for slot in (1, 7, 0):
        sibling_rows(slot)

    def y_second(a, i):
        xs = order[a]
        for way, slot in ((0, 1), (1, 3)):
            j = 2 * way + i
            arrived(yr1.at[a, j], ry1_sem.at[a, j])
            tgrad[slot, xs, j] = (tgrad[slot, xs, j].astype(F32) + yr1[a, j].astype(F32)).astype(BF16)
            send(tgrad.at[slot, xs, j], yr2.at[a, way, j], ry2_sem.at[a, way, j], yn[way])

    def z_next(far, other):
        for way in (0, 1):
            z_send(way, far, 1 - way if other else way)

    settle(gathered)
    z_next(3, False)
    y_second(1, 0)
    sibling_here(2, 6, 1, 7, 0)
    z_next(2, True)
    y_second(1, 1)
    z_next(2, False)
    y_second(0, 0)
    z_next(1, True)
    y_second(0, 1)

    def y_total(a, j):
        for way in (0, 1):
            arrived(yr2.at[a, way, j], ry2_sem.at[a, way, j])
        rows = pl.ds(pl.multiple_of(order[a] * OWN + j * QUARTER, QUARTER), QUARTER)
        return town[rows, :] + yr2[a, 0, j].astype(F32) + yr2[a, 1, j].astype(F32)

    def dx_copy(j):
        part = pl.ds(j * QUARTER, QUARTER)
        return copy(dfull.at[mp, part], dfull.at[mp, part], dx_sem.at[j], xl)

    def backward(j):
        part = pl.ds(j * QUARTER, QUARTER)
        unit_v = unit[part, :]
        grad_v = grad[part, :]
        dproj = (grad_v - unit_v * jnp.sum(unit_v * grad_v, axis=-1, keepdims=True)) * inv_s[part, :]
        dfull[mp, part] = dproj.astype(BF16)
        dx_copy(j).start()

    def second_sum(j):
        xsend[1, j] = y_total(1, j).astype(BF16)
        send(xsend.at[1, j], xl_recv.at[j], rx_sem.at[j], xl)

    def first_sum(j):
        value = y_total(0, j)
        arrived(xl_recv.at[j], rx_sem.at[j])
        return value + xl_recv[j].astype(F32)

    def image_sum(ch):
        rows = pl.ds(ch * QUARTER, QUARTER)
        value = igrad[rows, :] + sib_recv[0, rows, :].astype(F32)
        for way in (0, 1):
            arrived(zrecv.at[way, 0, ch], rz_sem.at[way, 0, ch])
            value = value + zrecv[way, 0, ch].astype(F32)
        return value

    def first_out(j):
        xsend[0, j] = first_sum(j).astype(BF16)
        send(xsend.at[0, j], xr_recv.at[j], rr_sem.at[j], xr, is_image)

    def image_out(ch):
        ib_send[ch] = image_sum(ch).astype(BF16)
        send(ib_send.at[ch], ib_recv.at[ch], ib_sem.at[ch], xr, is_home)

    second_sum(0)
    second_sum(2)
    z_next(1, False)
    second_sum(1)
    second_sum(3)

    def image_tail():
        first_out(0)
        first_out(2)
        for ch in (0, 1):
            grad[pl.ds(ch * QUARTER, QUARTER), :] = image_sum(ch)
            backward(ch)
        first_out(1)
        first_out(3)
        for ch in (0, 1):
            arrived(ib_recv.at[ch], ib_sem.at[ch])
            grad[pl.ds(HALF + ch * QUARTER, QUARTER), :] = ib_recv[ch].astype(F32)
            backward(2 + ch)

    def text_tail():
        grad[pl.ds(0, QUARTER), :] = first_sum(0)
        image_out(0)
        image_out(1)
        for j in (2, 1, 3):
            grad[pl.ds(j * QUARTER, QUARTER), :] = first_sum(j)
        for j in RTURN:
            arrived(xr_recv.at[j], rr_sem.at[j])
            rows = pl.ds(j * QUARTER, QUARTER)
            grad[rows, :] = grad[rows, :] + xr_recv[j].astype(F32)
            backward(j)

    only(is_image, image_tail)
    only(is_home, text_tail)
    for j in range(4):
        sent.append((is_image, copy(xsend.at[0, j], xr_recv.at[j], rr_sem.at[j], xr)))
    for ch in (0, 1):
        sent.append((is_home, copy(ib_send.at[ch], ib_recv.at[ch], ib_sem.at[ch], xr)))

    settle(len(sent) - 10)
    for j in range(4):
        sent.append((None, dx_copy(j)))
    for j in range(4):
        part = pl.ds(j * QUARTER, QUARTER)
        arrived(dfull.at[1 - mp, part], dx_sem.at[j])
    dproj_all = dfull[...].reshape(ROWS, E)

    theirs_l = pl.ds(pl.multiple_of((1 - c) * LANES, LANES), LANES)
    mine_l = pl.ds(pl.multiple_of(c * LANES, LANES), LANES)
    for l in range(3):
        local[l] = dot(dproj_all, normed[:, l * 2 * LANES:(l + 1) * 2 * LANES], TN)
        c_send[l] = local[l, :, theirs_l].astype(BF16)
        send(c_send.at[l], c_recv.at[l], c_sem.at[l], sib)

    dnormed = dot(dproj_all, weight[0])
    gin_out[0] = (dnormed / rms_s[...]).astype(BF16)

    settle(len(sent) - 3)
    EH = EY // 2

    def w_part(l, r, h):
        rows = pl.ds(pl.multiple_of(((y + r) % NY) * EY + h * EH, EH), EH)
        return local[l, rows, mine_l] + c_recv[l, rows, :].astype(F32)

    for l in range(3):
        arrived(c_recv.at[l], c_sem.at[l])
        for way in (0, 1):
            wy_send[l, way, 2] = w_part(l, 2, way).astype(BF16)
            send(wy_send.at[l, way, 2], wy_r1.at[l, way], wy1_sem.at[l, way], yn[way])
        for way, r in ((0, 1), (1, 3)):
            wy_send[l, way, 1 - way] = w_part(l, r, 1 - way).astype(BF16)
            send(wy_send.at[l, way, 1 - way], wy_r2.at[l, way, 1 - way], wy2_sem.at[l, way, 1 - way], yn[way])
    for l in range(3):
        for way, r in ((0, 1), (1, 3)):
            arrived(wy_r1.at[l, way], wy1_sem.at[l, way])
            wy_send[l, way, way] = (w_part(l, r, way) + wy_r1[l, way].astype(F32)).astype(BF16)
            send(wy_send.at[l, way, way], wy_r2.at[l, way, way], wy2_sem.at[l, way, way], yn[way])
    settle(len(sent) - 18)
    out_row = lax.broadcasted_iota(jnp.int32, (NZ * 48, EY), 0)
    in_row = lax.broadcasted_iota(jnp.int32, (NZ * 48, EY), 1)
    group = out_row // 24
    inner = out_row - group * 24
    spread = jnp.where(jnp.logical_and(inner < 18, in_row == group * 18 + inner), 1.0, 0.0).astype(BF16)
    for l in range(3):
        total = []
        for h in (0, 1):
            value = w_part(l, 0, h)
            for way in (0, 1):
                arrived(wy_r2.at[l, way, h], wy2_sem.at[l, way, h])
                value = value + wy_r2[l, way, h].astype(F32)
            total.append(value.astype(BF16))
        total = jnp.concatenate(total, axis=0)
        wz_send[l] = dot(spread, total).astype(BF16).reshape(NZ, 48, LANES)
        for d in range(1, NZ):
            send(wz_send.at[l, (z + d) % NZ], wz_recv.at[l, d], wz_sem.at[l, d], zs[d])
    settle(len(sent) - 21)
    for l in range(3):
        value = wz_send[l, z].astype(F32)
        for d in range(1, NZ):
            arrived(wz_recv.at[l, d], wz_sem.at[l, d])
            value = value + wz_recv[l, d].astype(F32)
        wc_send[l] = value.reshape(2, 24, LANES)
        send(wc_send.at[l, 1 - c], wc_recv.at[l], wc_sem.at[l], sib)
        gw_out[0, :, pl.ds(pl.multiple_of((2 * l + c) * LANES, LANES), LANES)] = wc_send[l, c, :18, :]
    for l in range(3):
        arrived(wc_recv.at[l], wc_sem.at[l])
        gw_out[0, :, pl.ds(pl.multiple_of((2 * l + 1 - c) * LANES, LANES), LANES)] = wc_recv[l, :18, :]

    settle(len(sent))


def scratch():
    vmem, dma = pltpu.VMEM, pltpu.SemaphoreType.DMA
    return [
        vmem((ROWS, DH), BF16), vmem((ROWS, 1), F32), vmem((4, QUARTER, E), BF16), vmem((4, QUARTER, E), BF16),
        vmem((OWN, E), F32), vmem((OWN, E), F32), vmem((OWN, 1), F32), vmem((2, QUARTER, E), BF16),
        vmem((NZ, 2, 2, QUARTER, E), BF16), vmem((NY, 2, 4, QUARTER, E), BF16),
        vmem((NZ * OWN, E), F32), vmem((NY, 2, 4, QUARTER, E), BF16), vmem((NZ * OWN, NY * ROWS), BF16), vmem((ROWS, E), F32), vmem((2, ROWS, E), F32),
        vmem((NZ, HALF, E), BF16), vmem((NZ, HALF, E), BF16),
        vmem((2, 4, 2, QUARTER, E), BF16), vmem((2, 4, 2, QUARTER, E), BF16),
        vmem((2, 4, QUARTER, E), BF16), vmem((2, 2, 4, QUARTER, E), BF16),
        vmem((2, 4, QUARTER, E), BF16), vmem((4, QUARTER, E), BF16), vmem((4, QUARTER, E), BF16),
        vmem((2, QUARTER, E), BF16), vmem((2, QUARTER, E), BF16),
        vmem((OWN, E), F32), vmem((2, OWN, E), BF16),
        vmem((3, E, 2 * LANES), F32), vmem((3, E, LANES), BF16), vmem((3, E, LANES), BF16),
        vmem((3, 2, 3, EY // 2, LANES), BF16), vmem((3, 2, EY // 2, LANES), BF16), vmem((3, 2, 2, EY // 2, LANES), BF16),
        vmem((3, NZ, 48, LANES), BF16), vmem((3, NZ, 48, LANES), BF16),
        vmem((3, 2, 24, LANES), F32), vmem((3, 24, LANES), F32),
        dma((4, 2)), dma((2, 2)), dma((4, 2, 2, 2)), dma((NZ, 2, 2)), dma((4, 2, 2)), dma((2, 4, 2, 2)),
        dma((2, 4, 2)),
        dma((NZ, 2)), dma((2, 4, 2, 2)), dma((2, 4, 2)), dma((2, 2, 4, 2)), dma((4, 2)), dma((4, 2)),
        dma((2, 2)), dma((4, 2)),
        dma((3, 2)), dma((3, 2, 2)), dma((3, 2, 2, 2)), dma((3, NZ, 2)), dma((3, 2)),
    ]


def shards(inputs, head_weight, pair_index):
    space = pl.BlockSpec(memory_space=pltpu.VMEM)
    return pl.pallas_call(
        kernel,
        out_shape=(
            jax.ShapeDtypeStruct((1, E // 64, DH), F32),
            jax.ShapeDtypeStruct((1, ROWS, DH), BF16),
        ),
        in_specs=[space] * 3,
        out_specs=(space, space),
        scratch_shapes=scratch(),
        compiler_params=pltpu.CompilerParams(
            collective_id=0, has_side_effects=True, vmem_limit_bytes=60 * 2**20
        ),
    )(inputs, head_weight, pair_index.reshape(2, OWN))


def solution(mesh):
    in_specs = (P("tower", "dp", None), P("tower", None, "mp"), P("dp"))
    out_specs = (P("tower", "dp", "mp"), P("tower", "dp", "mp"))
    return jax.shard_map(shards, mesh=mesh, in_specs=in_specs, out_specs=out_specs, check_vma=False)
```

time: 110 us -> 106 us (0.964)
  Pallas kernels: 106 us -> 101 us
    pallas_call x1, Pallas kernels: 106 us -> 101 us  [shards(): pl.pallas_call(kernel, out_shape=(jax.ShapeDtypeStruct((1, E // 64, DH),...]
where the time goes in v3:
time: 106 us; the launch traced here: 105 us
  Pallas kernels  101 us (95%)
  local copies, waits for them, and re-layouts  3.33 us (3%)
    pallas_call x1, Pallas kernels, shards(): pl.pallas_call(kernel, out_shape=(jax.ShapeDtypeStruct((1, E // 64, DH),...  101 us

profile of v3, /device:TPU:5, one launch (start us, length us, event | category | flops | bytes accessed | tf_op | source)
XLA Modules:
  0.0 105.3 jit_solution(12875468563049248434)
XLA Ops:
  0.6 101.3 %shard_map.50 = (f32[1,18,768]{2,1,0:T(8,128)}, bf16[1,256,768]{2,1,0:T(8,128)(2,1)}) custom-call(bf16[1,256,1536]{2,1,0:T(8,128)(2,1)} %pooled.1, bf16[1,1152,768]{2,1,0:T(8,128)(2,1)} %weight.1, s32[2,128]{1,0:T(2,128)} %bitcast.1), custom_call_target="tpu_custom_call" | custom-call | tf_op jit(solution)/shard_map/pallas_call | solution.py:559
  102.0 1.6 %copy.5 = f32[1,18,768]{2,0,1:T(1,128)} copy(f32[1,18,768]{2,1,0:T(8,128)} %get-tuple-element.2) | data formatting | bytes 110592 | tf_op jit(solution)/shard_map/pallas_call | solution.py:559
  103.5 1.8 %copy.7 = bf16[1,256,768]{2,1,0:T(8,128)(2,1)} copy(bf16[1,256,768]{2,1,0:T(8,128)(2,1)} %get-tuple-element.7) | data formatting | bytes 786432

commit v4 on v3

--- a/solution.py
+++ b/solution.py
@@ -41,11 +41,11 @@
     pooled, weight, pairs, gw_out, gin_out,
     normed, rms_s, hsend, hrecv, proj, unit, inv_s, ebuf,
     img, txt, igrad, tgrad, coef, town, beside,
-    sib_send, sib_recv, zsend, zrecv, yr1, yr2, xsend, xl_recv, xr_recv, ib_send, ib_recv,
+    sib_send, sib_recv, zsend, zrecv, two_recv, yr1, yr2, xsend, xl_recv, xr_recv, ib_send, ib_recv,
     grad, dfull,
     local, c_send, c_recv, wy_send, wy_r1, wy_r2, wz_send, wz_recv, wc_send, wc_recv,
     h_sem, ix_sem, zr_sem, sb_sem, tx_sem, ty_sem, tf_sem,
-    rsb_sem, rz_sem, ry1_sem, ry2_sem, rx_sem, rr_sem, ib_sem, dx_sem,
+    rsb_sem, rz_sem, two_sem, ry1_sem, ry2_sem, rx_sem, rr_sem, ib_sem, dx_sem,
     c_sem, wy1_sem, wy2_sem, wz_sem, wc_sem,
 ):
     dp = lax.axis_index("dp")
@@ -199,8 +199,12 @@
         xs = order[a]
         for way, slot in ((0, 3), (1, 1)):
             arrived(txt.at[slot, xs, j], ty_sem.at[a, j, way])
-            if j // 2 == way:
-                send(txt.at[slot, xs, j], txt.at[2, xs, j], tf_sem.at[a, j], yn[way])
+            if a == 0 and j // 2 == way:
+                send(txt.at[slot, xs, j], txt.at[2, xs, j], tf_sem.at[0, j], yn[way])
+
+    def two_away(j):
+        arrived(txt.at[2, first, j], tf_sem.at[0, j])
+        send(txt.at[2, first, j], txt.at[2, first, j], tf_sem.at[1, j], xl)
 
     def first_here(j):
         arrived(txt.at[0, first, j], tx_sem.at[j, 0])
@@ -288,11 +292,15 @@
     ring(3, 0)
     y_forward(1, 3)
     ring(3, 1)
+    two_away(2)
+    two_away(3)
     y_forward(1, 0)
     y_forward(1, 1)
     sibling_images(0, 5)
     town[...] = block(0, 0, 5, masked=True)
+    two_away(0)
     ring(4, 0)
+    two_away(1)
     beside[0] = block(1, 0, 5)
     ring(4, 1)
     beside[1] = block(3, 0, 5)
@@ -302,13 +310,12 @@
 
     for way, slot in ((0, 1), (1, 3)):
         tgrad[slot] = (beside[way] + block(slot, 5, 8)).astype(BF16).reshape(2, 4, QUARTER, E)
-        for a in (1, 0):
-            for j in (2 - 2 * way, 3 - 2 * way):
+        for a, chunks in ((1, RTURN), (0, (2 - 2 * way, 3 - 2 * way))):
+            for j in chunks:
                 send(tgrad.at[slot, order[a], j], yr2.at[a, way, j], ry2_sem.at[a, way, j], yn[way])
 
-    for a in (0, 1):
-        for j in range(4):
-            arrived(txt.at[2, order[a], j], tf_sem.at[a, j])
+    for j in range(4):
+        arrived(txt.at[2, second, j], tf_sem.at[1, j])
 
     def sibling_rows(slot):
         p = POS[slot]
@@ -331,11 +338,8 @@
             arrived(sib_recv.at[POS[slot]], rsb_sem.at[POS[slot]])
 
     tgrad[2] = block(2, 0, NZ).astype(BF16).reshape(2, 4, QUARTER, E)
-    for a in (1, 0):
-        for i in (0, 1):
-            for way in (0, 1):
-                j = 2 * way + i
-                send(tgrad.at[2, order[a], j], yr1.at[a, j], ry1_sem.at[a, j], yn[way])
+    for j in RTURN:
+        send(tgrad.at[2, second, j], two_recv.at[j], two_sem.at[j], xl)
 
     town[...] += block(0, 5, 8)
     image_block(5, 8)
@@ -349,33 +353,26 @@
         z_send(way, 4, way)
     for way in (0, 1):
         z_send(way, 3, 1 - way)
+    for j in RTURN:
+        arrived(two_recv.at[j], two_sem.at[j])
+        tgrad[2, first, j] = (tgrad[2, first, j].astype(F32) + two_recv[j].astype(F32)).astype(BF16)
+        send(tgrad.at[2, first, j], yr1.at[j], ry1_sem.at[j], yn[j // 2])
     image_block(0, 3)
     for slot in (1, 7, 0):
         sibling_rows(slot)
 
-    def y_second(a, i):
-        xs = order[a]
+    def y_second(i):
         for way, slot in ((0, 1), (1, 3)):
             j = 2 * way + i
-            arrived(yr1.at[a, j], ry1_sem.at[a, j])
-            tgrad[slot, xs, j] = (tgrad[slot, xs, j].astype(F32) + yr1[a, j].astype(F32)).astype(BF16)
-            send(tgrad.at[slot, xs, j], yr2.at[a, way, j], ry2_sem.at[a, way, j], yn[way])
+            arrived(yr1.at[j], ry1_sem.at[j])
+            tgrad[slot, first, j] = (tgrad[slot, first, j].astype(F32) + yr1[j].astype(F32)).astype(BF16)
+            send(tgrad.at[slot, first, j], yr2.at[0, way, j], ry2_sem.at[0, way, j], yn[way])
 
     def z_next(far, other):
         for way in (0, 1):
             z_send(way, far, 1 - way if other else way)
 
     settle(gathered)
-    z_next(3, False)
-    y_second(1, 0)
-    sibling_here(2, 6, 1, 7, 0)
-    z_next(2, True)
-    y_second(1, 1)
-    z_next(2, False)
-    y_second(0, 0)
-    z_next(1, True)
-    y_second(0, 1)
-
     def y_total(a, j):
         for way in (0, 1):
             arrived(yr2.at[a, way, j], ry2_sem.at[a, way, j])
@@ -419,11 +416,18 @@
         ib_send[ch] = image_sum(ch).astype(BF16)
         send(ib_send.at[ch], ib_recv.at[ch], ib_sem.at[ch], xr, is_home)
 
+    z_next(3, False)
     second_sum(0)
     second_sum(2)
-    z_next(1, False)
+    sibling_here(2, 6, 1, 7, 0)
+    z_next(2, True)
     second_sum(1)
     second_sum(3)
+    y_second(0)
+    z_next(2, False)
+    y_second(1)
+    z_next(1, True)
+    z_next(1, False)
 
     def image_tail():
         first_out(0)
@@ -511,7 +515,7 @@
             total.append(value.astype(BF16))
         total = jnp.concatenate(total, axis=0)
         wz_send[l] = dot(spread, total).astype(BF16).reshape(NZ, 48, LANES)
-        for d in range(1, NZ):
+        for d in (4, 3, 5, 2, 6, 1, 7):
             send(wz_send.at[l, (z + d) % NZ], wz_recv.at[l, d], wz_sem.at[l, d], zs[d])
     settle(len(sent) - 21)
     for l in range(3):
@@ -529,6 +533,11 @@
     settle(len(sent))
 
 
+def finish(head, pooled, head_out, pooled_out):
+    head_out[:, 0, :] = head[0]
+    pooled_out[...] = pooled[...]
+
+
 def scratch():
     vmem, dma = pltpu.VMEM, pltpu.SemaphoreType.DMA
     return [
@@ -538,7 +547,7 @@
         vmem((NZ * OWN, E), F32), vmem((NY, 2, 4, QUARTER, E), BF16), vmem((NZ * OWN, NY * ROWS), BF16), vmem((ROWS, E), F32), vmem((2, ROWS, E), F32),
         vmem((NZ, HALF, E), BF16), vmem((NZ, HALF, E), BF16),
         vmem((2, 4, 2, QUARTER, E), BF16), vmem((2, 4, 2, QUARTER, E), BF16),
-        vmem((2, 4, QUARTER, E), BF16), vmem((2, 2, 4, QUARTER, E), BF16),
+        vmem((4, QUARTER, E), BF16), vmem((4, QUARTER, E), BF16), vmem((2, 2, 4, QUARTER, E), BF16),
         vmem((2, 4, QUARTER, E), BF16), vmem((4, QUARTER, E), BF16), vmem((4, QUARTER, E), BF16),
         vmem((2, QUARTER, E), BF16), vmem((2, QUARTER, E), BF16),
         vmem((OWN, E), F32), vmem((2, OWN, E), BF16),
@@ -548,7 +557,7 @@
         vmem((3, 2, 24, LANES), F32), vmem((3, 24, LANES), F32),
         dma((4, 2)), dma((2, 2)), dma((4, 2, 2, 2)), dma((NZ, 2, 2)), dma((4, 2, 2)), dma((2, 4, 2, 2)),
         dma((2, 4, 2)),
-        dma((NZ, 2)), dma((2, 4, 2, 2)), dma((2, 4, 2)), dma((2, 2, 4, 2)), dma((4, 2)), dma((4, 2)),
+        dma((NZ, 2)), dma((2, 4, 2, 2)), dma((4, 2)), dma((4, 2)), dma((2, 2, 4, 2)), dma((4, 2)), dma((4, 2)),
         dma((2, 2)), dma((4, 2)),
         dma((3, 2)), dma((3, 2, 2)), dma((3, 2, 2, 2)), dma((3, NZ, 2)), dma((3, 2)),
     ]
@@ -556,7 +565,7 @@
 
 def shards(inputs, head_weight, pair_index):
     space = pl.BlockSpec(memory_space=pltpu.VMEM)
-    return pl.pallas_call(
+    grads = pl.pallas_call(
         kernel,
         out_shape=(
             jax.ShapeDtypeStruct((1, E // 64, DH), F32),
@@ -569,6 +578,16 @@
             collective_id=0, has_side_effects=True, vmem_limit_bytes=60 * 2**20
         ),
     )(inputs, head_weight, pair_index.reshape(2, OWN))
+    head, pooled = pl.pallas_call(
+        finish,
+        out_shape=(
+            jax.ShapeDtypeStruct((E // 64, 1, DH), F32),
+            jax.ShapeDtypeStruct((1, ROWS, DH), BF16),
+        ),
+        in_specs=[space] * 2,
+        out_specs=(space, space),
+    )(*grads)
+    return head.reshape(1, E // 64, DH), pooled
 
 
 def solution(mesh):

time: 106 us -> 103 us (0.972)
  local copies, waits for them, and re-layouts: 3.33 us -> 0 us
    pallas_call x1, Pallas kernels: 101 us -> 99 us  [shards(): pl.pallas_call(kernel, out_shape=(jax.ShapeDtypeStruct((1, E // 64, DH),...]
    pallas_call x0 -> x1, Pallas kernels: none -> 1.83 us  [shards(): pl.pallas_call(finish, out_shape=(jax.ShapeDtypeStruct((E // 64, 1, DH),...]
    unnamed x1 -> x0, local copies, waits for them, and re-layouts: 1.77 us -> none
    pallas_call x1 -> x0, local copies, waits for them, and re-layouts: 1.56 us -> none  [shards(): pl.pallas_call(kernel, out_shape=(jax.ShapeDtypeStruct((1, E // 64, DH),...]
where the time goes in v4:
time: 103 us; the launch traced here: 101 us
  Pallas kernels  101 us (98%)
    pallas_call x1, Pallas kernels, shards(): pl.pallas_call(kernel, out_shape=(jax.ShapeDtypeStruct((1, E // 64, DH),...  99 us

profile of v4, /device:TPU:5, one launch (start us, length us, event | category | flops | bytes accessed | tf_op | source)
XLA Modules:
  0.0 101.4 jit_solution(4582563555772994837)
XLA Ops:
  0.6 99.0 %shard_map.50 = (f32[1,18,768]{2,1,0:T(8,128)}, bf16[1,256,768]{2,1,0:T(8,128)(2,1)}) custom-call(bf16[1,256,1536]{2,1,0:T(8,128)(2,1)} %pooled.1, bf16[1,1152,768]{2,1,0:T(8,128)(2,1)} %weight.1, s32[2,128]{1,0:T(2,128)} %bitcast.2), custom_call_target="tpu_custom_call" | custom-call | tf_op jit(solution)/shard_map/pallas_call | solution.py:568
  99.6 1.8 %shard_map.51 = (f32[18,1,768]{2,1,0:T(1,128)}, bf16[1,256,768]{2,1,0:T(8,128)(2,1)}) custom-call(f32[1,18,768]{2,1,0:T(8,128)} %get-tuple-element.6.head, bf16[1,256,768]{2,1,0:T(8,128)(2,1)} %get-tuple-element.7.pooled), custom_call_target="tpu_custom_call" | custom-call | tf_op jit(solution)/shard_map/pallas_call | solution.py:581

commit v5 on v4

--- a/solution.py
+++ b/solution.py
@@ -38,7 +38,8 @@
 
 
 def kernel(
-    pooled, weight, pairs, gw_out, gin_out,
+    pooled_in, weight_in, pairs, gw_out, gin_out,
+    pooled, weight, load_sem,
     normed, rms_s, hsend, hrecv, proj, unit, inv_s, ebuf,
     img, txt, igrad, tgrad, coef, town, beside,
     sib_send, sib_recv, zsend, zrecv, two_recv, yr1, yr2, xsend, xl_recv, xr_recv, ib_send, ib_recv,
@@ -76,6 +77,11 @@
     for peer in peers:
         pl.semaphore_signal(barrier, inc=1, device_id=peer, device_id_type=MESH)
 
+    load_pooled = pltpu.make_async_copy(pooled_in, pooled, load_sem.at[0])
+    load_weight = pltpu.make_async_copy(weight_in, weight, load_sem.at[1])
+    load_pooled.start()
+    load_weight.start()
+
     sent = []
     mode = {"run": True, "keep": True}
 
@@ -119,6 +125,7 @@
         work()
         mode["run"] = True
 
+    load_pooled.wait()
     full = pooled[0].astype(F32)
     rms = jnp.sqrt(jnp.mean(full * full, axis=-1, keepdims=True) + EPSILON)
     rms_s[...] = rms
@@ -126,6 +133,7 @@
     normed[...] = (part / rms).astype(BF16)
     theirs = pl.ds(pl.multiple_of((1 - mp) * OWN, OWN), OWN)
     mine = pl.ds(pl.multiple_of(mp * OWN, OWN), OWN)
+    load_weight.wait()
     hsend[...] = dot(normed[theirs, :], weight[0], NT).astype(BF16).reshape(4, QUARTER, E)
     pl.semaphore_wait(barrier, len(peers))
     for j in TURN:
@@ -292,16 +300,16 @@
     ring(3, 0)
     y_forward(1, 3)
     ring(3, 1)
-    two_away(2)
-    two_away(3)
     y_forward(1, 0)
     y_forward(1, 1)
     sibling_images(0, 5)
     town[...] = block(0, 0, 5, masked=True)
+    two_away(2)
+    two_away(3)
+    ring(4, 0)
+    beside[0] = block(1, 0, 5)
     two_away(0)
-    ring(4, 0)
     two_away(1)
-    beside[0] = block(1, 0, 5)
     ring(4, 1)
     beside[1] = block(3, 0, 5)
     sibling_images(5, 8)
@@ -541,6 +549,7 @@
 def scratch():
     vmem, dma = pltpu.VMEM, pltpu.SemaphoreType.DMA
     return [
+        vmem((1, ROWS, D), BF16), vmem((1, E, DH), BF16), dma((2,)),
         vmem((ROWS, DH), BF16), vmem((ROWS, 1), F32), vmem((4, QUARTER, E), BF16), vmem((4, QUARTER, E), BF16),
         vmem((OWN, E), F32), vmem((OWN, E), F32), vmem((OWN, 1), F32), vmem((2, QUARTER, E), BF16),
         vmem((NZ, 2, 2, QUARTER, E), BF16), vmem((NY, 2, 4, QUARTER, E), BF16),
@@ -571,7 +580,7 @@
             jax.ShapeDtypeStruct((1, E // 64, DH), F32),
             jax.ShapeDtypeStruct((1, ROWS, DH), BF16),
         ),
-        in_specs=[space] * 3,
+        in_specs=[pl.BlockSpec(memory_space=pl.ANY)] * 2 + [space],
         out_specs=(space, space),
         scratch_shapes=scratch(),
         compiler_params=pltpu.CompilerParams(

time: 103 us -> 101 us (0.981)
  Pallas kernels: 101 us -> 99.3 us
    pallas_call x1, Pallas kernels: 99 us -> 97.4 us  [shards(): pl.pallas_call(kernel, out_shape=(jax.ShapeDtypeStruct((1, E // 64, DH),...]
where the time goes in v5:
time: 101 us; the launch traced here: 99.9 us
  Pallas kernels  99.3 us (98%)
    pallas_call x1, Pallas kernels, shards(): pl.pallas_call(kernel, out_shape=(jax.ShapeDtypeStruct((1, E // 64, DH),...  97.4 us

profile of v5, /device:TPU:5, one launch (start us, length us, event | category | flops | bytes accessed | tf_op | source)
XLA Modules:
  0.0 99.9 jit_solution(9403445950266386075)
XLA Ops:
  0.6 97.4 %shard_map.50 = (f32[1,18,768]{2,1,0:T(8,128)}, bf16[1,256,768]{2,1,0:T(8,128)(2,1)}) custom-call(bf16[1,256,1536]{2,1,0:T(8,128)(2,1)} %pooled_in.1, bf16[1,1152,768]{2,1,0:T(8,128)(2,1)} %weight_in.1, s32[2,128]{1,0:T(2,128)} %bitcast.2), custom_call_target="tpu_custom_call" | custom-call | tf_op jit(solution)/shard_map/pallas_call | solution.py:577
  98.1 1.8 %shard_map.51 = (f32[18,1,768]{2,1,0:T(1,128)}, bf16[1,256,768]{2,1,0:T(8,128)(2,1)}) custom-call(f32[1,18,768]{2,1,0:T(8,128)} %get-tuple-element.6.head, bf16[1,256,768]{2,1,0:T(8,128)(2,1)} %get-tuple-element.7.pooled), custom_call_target="tpu_custom_call" | custom-call | tf_op jit(solution)/shard_map/pallas_call | solution.py:590

commit v6 on v5

--- a/solution.py
+++ b/solution.py
@@ -39,7 +39,7 @@
 
 def kernel(
     pooled_in, weight_in, pairs, gw_out, gin_out,
-    pooled, weight, load_sem,
+    pooled, weight, gin, load_sem,
     normed, rms_s, hsend, hrecv, proj, unit, inv_s, ebuf,
     img, txt, igrad, tgrad, coef, town, beside,
     sib_send, sib_recv, zsend, zrecv, two_recv, yr1, yr2, xsend, xl_recv, xr_recv, ib_send, ib_recv,
@@ -485,7 +485,9 @@
         send(c_send.at[l], c_recv.at[l], c_sem.at[l], sib)
 
     dnormed = dot(dproj_all, weight[0])
-    gin_out[0] = (dnormed / rms_s[...]).astype(BF16)
+    gin[0] = (dnormed / rms_s[...]).astype(BF16)
+    store_gin = pltpu.make_async_copy(gin, gin_out, load_sem.at[2])
+    store_gin.start()
 
     settle(len(sent) - 3)
     EH = EY // 2
@@ -538,18 +540,21 @@
         arrived(wc_recv.at[l], wc_sem.at[l])
         gw_out[0, :, pl.ds(pl.multiple_of((2 * l + 1 - c) * LANES, LANES), LANES)] = wc_recv[l, :18, :]
 
+    store_gin.wait()
     settle(len(sent))
 
 
-def finish(head, pooled, head_out, pooled_out):
+def finish(head, pooled, head_out, pooled_out, sem):
+    step = pltpu.make_async_copy(pooled, pooled_out, sem)
+    step.start()
     head_out[:, 0, :] = head[0]
-    pooled_out[...] = pooled[...]
+    step.wait()
 
 
 def scratch():
     vmem, dma = pltpu.VMEM, pltpu.SemaphoreType.DMA
     return [
-        vmem((1, ROWS, D), BF16), vmem((1, E, DH), BF16), dma((2,)),
+        vmem((1, ROWS, D), BF16), vmem((1, E, DH), BF16), vmem((1, ROWS, DH), BF16), dma((3,)),
         vmem((ROWS, DH), BF16), vmem((ROWS, 1), F32), vmem((4, QUARTER, E), BF16), vmem((4, QUARTER, E), BF16),
         vmem((OWN, E), F32), vmem((OWN, E), F32), vmem((OWN, 1), F32), vmem((2, QUARTER, E), BF16),
         vmem((NZ, 2, 2, QUARTER, E), BF16), vmem((NY, 2, 4, QUARTER, E), BF16),
@@ -581,7 +586,7 @@
             jax.ShapeDtypeStruct((1, ROWS, DH), BF16),
         ),
         in_specs=[pl.BlockSpec(memory_space=pl.ANY)] * 2 + [space],
-        out_specs=(space, space),
+        out_specs=(space, pl.BlockSpec(memory_space=pl.ANY)),
         scratch_shapes=scratch(),
         compiler_params=pltpu.CompilerParams(
             collective_id=0, has_side_effects=True, vmem_limit_bytes=60 * 2**20
@@ -593,8 +598,9 @@
             jax.ShapeDtypeStruct((E // 64, 1, DH), F32),
             jax.ShapeDtypeStruct((1, ROWS, DH), BF16),
         ),
-        in_specs=[space] * 2,
-        out_specs=(space, space),
+        in_specs=[space, pl.BlockSpec(memory_space=pl.ANY)],
+        out_specs=(space, pl.BlockSpec(memory_space=pl.ANY)),
+        scratch_shapes=[pltpu.SemaphoreType.DMA],
     )(*grads)
     return head.reshape(1, E // 64, DH), pooled
 

time: 101 us -> 114 us (1.13)
  Pallas kernels: 99.3 us -> 112 us
    pallas_call x1, Pallas kernels: 1.83 us -> 14.5 us  [shards(): pl.pallas_call(finish, out_shape=(jax.ShapeDtypeStruct((E // 64, 1, DH),...]
where the time goes in v6:
time: 114 us; the launch traced here: 113 us
  Pallas kernels  112 us (98%)
    pallas_call x1, Pallas kernels, shards(): pl.pallas_call(kernel, out_shape=(jax.ShapeDtypeStruct((1, E // 64, DH),...  97.3 us
    pallas_call x1, Pallas kernels, shards(): pl.pallas_call(finish, out_shape=(jax.ShapeDtypeStruct((E // 64, 1, DH),...  14.5 us

profile of v6, /device:TPU:5, one launch (start us, length us, event | category | flops | bytes accessed | tf_op | source)
XLA Modules:
  0.0 112.6 jit_solution(16166457815376958298)
XLA Ops:
  0.6 97.3 %shard_map.50 = (f32[1,18,768]{2,1,0:T(8,128)}, bf16[1,256,768]{2,1,0:T(8,128)(2,1)}) custom-call(bf16[1,256,1536]{2,1,0:T(8,128)(2,1)} %pooled_in.1, bf16[1,1152,768]{2,1,0:T(8,128)(2,1)} %weight_in.1, s32[2,128]{1,0:T(2,128)} %bitcast.2), custom_call_target="tpu_custom_call" | custom-call | tf_op jit(solution)/shard_map/pallas_call | solution.py:582
  97.9 14.5 %shard_map.51 = (f32[18,1,768]{2,1,0:T(1,128)}, bf16[1,256,768]{2,1,0:T(8,128)(2,1)}) custom-call(f32[1,18,768]{2,1,0:T(8,128)} %get-tuple-element.6.head, bf16[1,256,768]{2,1,0:T(8,128)(2,1)} %get-tuple-element.7.pooled), custom_call_target="tpu_custom_call" | custom-call | tf_op jit(solution)/shard_map/pallas_call | solution.py:595
